TPU v7x, 32 devices: a whole 2x2x4 slice. The times are simulated.
32 devices in a mesh: rows: 8 (over z, y), seq: 4 (over x, core).
Axes of the slice: x: 2, y: 2, z: 4, core: 2. Of those that a mesh axis runs over, the one named last changes fastest.
Arguments:
- tokens: bfloat16 [32, 512, 768], P('rows', 'seq'), may hold values from -6 to 6
- segment_ids: int32 [32, 512], P('rows', 'seq'), may hold values from 0 to 8, as said below
- w_query: bfloat16 [768, 768], replicated, may hold values from -0.21875 to 0.21875
- w_key: bfloat16 [768, 768], replicated, may hold values from -0.21875 to 0.21875
- w_value: bfloat16 [768, 768], replicated, may hold values from -0.21875 to 0.21875
- b_query: float32 [768], replicated, may hold values from -3 to 3
- b_value: float32 [768], replicated, may hold values from -3 to 3
- w_out: bfloat16 [768, 768], replicated, may hold values from -1.25 to 1.25
- b_out: float32 [768], replicated, may hold values from -3 to 3
- gain_attn: float32 [768], replicated, may hold values from 0.5 to 1.5
- shift_attn: float32 [768], replicated, may hold values from -3 to 3
- w_up: bfloat16 [768, 3072], replicated, may hold values from -0.21875 to 0.21875
- b_up: float32 [3072], replicated, may hold values from -3 to 3
- w_down: bfloat16 [3072, 768], replicated, may hold values from -0.109375 to 0.109375
- b_down: float32 [768], replicated, may hold values from -3 to 3
- gain_out: float32 [768], replicated, may hold values from 0.5 to 1.5
- shift_out: float32 [768], replicated, may hold values from -3 to 3
- token_cot: bfloat16 [32, 512, 768], P('rows', 'seq'), may hold values from -6 to 6
- pool_cot: float32 [32, 8, 1728], P('rows'), may hold values from -48 to 48
Outputs:
- layer_out: bfloat16 [32, 512, 768], P('rows', 'seq')
- pooled: float32 [32, 8, 1728], P('rows')
- grad_tokens: bfloat16 [32, 512, 768], P('rows', 'seq')
- grad_w_query: float32 [768, 768], P('rows')
- grad_w_key: float32 [768, 768], P('rows')
- grad_w_value: float32 [768, 768], P('rows')
- grad_b_query: float32 [768], P('rows')
- grad_b_value: float32 [768], P('rows')
- grad_w_out: float32 [768, 768], P('rows')
- grad_b_out: float32 [768], P('rows')
- grad_gain_attn: float32 [768], P('rows')
- grad_shift_attn: float32 [768], P('rows')
- grad_w_up: float32 [768, 3072], P('rows')
- grad_b_up: float32 [3072], P('rows')
- grad_w_down: float32 [3072, 768], P('rows')
- grad_b_down: float32 [768], P('rows')
- grad_gain_out: float32 [768], P('rows')
- grad_shift_out: float32 [768], P('rows')
Inputs may be any that keep to these rules, and one draw needn't show every extreme that they name: `segment_ids`: along each row the ids never fall; the id 8 marks padding, which only ends a row and takes at most 128 tokens; in each aligned block of 4 rows one row, drawn from the seed, is the single segment 0 without padding, and every other row ends in padding.
All inputs are finite; a program needn't handle non-finite values.
Results may differ from a plain program's by a relative error of at most 0.017.
Values may be sent and summed in bfloat16 or wider, within the bound.
No kernel may reach another device: no remote copies, remote signals or barrier semaphores. Data moves between devices by JAX's collectives and lax.ppermute only.
A program may use at most 128 MiB of HBM per device.

v0:
```python
import jax
import jax.numpy as jnp
from jax import lax
from jax.sharding import PartitionSpec as P

HEADS = 12
SEGS = 8


norm_eps = 1e-12
pool_eps = 1e-06
highest = lax.Precision.HIGHEST


def matmul(left, right):
    return jnp.dot(left, right, preferred_element_type=jnp.float32)


def layer_norm(hidden, gain_vec, shift_vec):
    centered = hidden - jnp.mean(hidden, axis=-1, keepdims=True)
    spread = jnp.mean(centered * centered, axis=-1, keepdims=True)
    return centered * lax.rsqrt(spread + norm_eps) * gain_vec + shift_vec


def exact_gelu(values_in):
    return jax.nn.gelu(values_in, approximate=False)


def pool_finish(seg_sums):
    width = seg_sums.shape[-1]
    pieces = []
    for keep_width in (width, width * 2 // 3, width // 3, width // 6, width // 12):
        window = seg_sums[..., :keep_width]
        factor = lax.rsqrt(jnp.mean(window * window, axis=-1, keepdims=True) + pool_eps)
        pieces.append(window * factor)
    return jnp.concatenate(pieces, axis=-1)


def split_heads(tensor, heads):
    return tensor.reshape(tensor.shape[0], tensor.shape[1], heads, tensor.shape[2] // heads)


def masked_scores(query_rows, key_rows, query_ids, key_ids, heads):
    score_scale = (query_rows.shape[-1] // heads) ** (-0.5)
    scores = (
        jnp.einsum(
            "nqhe,nkhe->nhqk",
            split_heads(query_rows, heads),
            split_heads(key_rows, heads),
            preferred_element_type=jnp.float32,
        )
        * score_scale
    )
    same_doc = query_ids[:, None, :, None] == key_ids[:, None, None, :]
    return jnp.where(same_doc, scores, -1e30)


def attend_forward(query_rows, key_rows, value_rows, query_ids, key_ids, heads):
    scores = masked_scores(query_rows, key_rows, query_ids, key_ids, heads)
    top_score = jnp.max(scores, axis=-1, keepdims=True)
    expo = jnp.exp(scores - top_score)
    total = jnp.sum(expo, axis=-1, keepdims=True)
    attn_probs = (expo / total).astype(jnp.bfloat16)
    mixed = jnp.einsum(
        "nhqk,nkhe->nqhe",
        attn_probs,
        split_heads(value_rows, heads),
        preferred_element_type=jnp.float32,
    )
    return (mixed.reshape(query_rows.shape), top_score + jnp.log(total))


def attend_backward(
    query_rows, key_rows, value_rows, query_ids, key_ids, log_total, grad_mixed, heads
):
    score_scale = (query_rows.shape[-1] // heads) ** (-0.5)
    scores = masked_scores(query_rows, key_rows, query_ids, key_ids, heads)
    attn_probs = jnp.exp(scores - log_total)
    grad_heads = split_heads(grad_mixed, heads)
    grad_probs = jnp.einsum(
        "nqhe,nkhe->nhqk",
        grad_heads,
        split_heads(value_rows, heads),
        preferred_element_type=jnp.float32,
    )
    inner = jnp.sum(attn_probs * grad_probs, axis=-1, keepdims=True)
    grad_scores = (attn_probs * (grad_probs - inner)).astype(jnp.bfloat16)
    grad_query = (
        jnp.einsum(
            "nhqk,nkhe->nqhe",
            grad_scores,
            split_heads(key_rows, heads),
            preferred_element_type=jnp.float32,
        )
        * score_scale
    )
    grad_keys = (
        jnp.einsum(
            "nhqk,nqhe->nkhe",
            grad_scores,
            split_heads(query_rows, heads),
            preferred_element_type=jnp.float32,
        )
        * score_scale
    )
    grad_values = jnp.einsum(
        "nhqk,nqhe->nkhe",
        attn_probs.astype(jnp.bfloat16),
        grad_heads,
        preferred_element_type=jnp.float32,
    )
    return (
        grad_query.reshape(query_rows.shape),
        grad_keys.reshape(key_rows.shape),
        grad_values.reshape(value_rows.shape),
    )


def transpose_dot(left, right):
    return jnp.einsum("tf,td->fd", left, right, preferred_element_type=jnp.float32)


def back_dot(grad_rows, weight):
    return jnp.einsum("td,fd->tf", grad_rows, weight, preferred_element_type=jnp.float32)


def local(
    tokens,
    segment_ids,
    w_query,
    w_key,
    w_value,
    b_query,
    b_value,
    w_out,
    b_out,
    gain_attn,
    shift_attn,
    w_up,
    b_up,
    w_down,
    b_down,
    gain_out,
    shift_out,
    token_cot,
    pool_cot,
):
    heads = HEADS
    width = tokens.shape[-1]
    local_tokens, local_cot, local_ids, local_pool_cot = (tokens, token_cot, segment_ids, pool_cot)
    seq_count, tok_count = local_ids.shape
    flat_rows = local_tokens.reshape(seq_count * tok_count, width)
    query_rows = (
        (matmul(flat_rows, w_query) + b_query)
        .astype(jnp.bfloat16)
        .reshape(seq_count, tok_count, width)
    )
    key_rows = matmul(flat_rows, w_key).astype(jnp.bfloat16).reshape(seq_count, tok_count, width)
    value_rows = (
        (matmul(flat_rows, w_value) + b_value)
        .astype(jnp.bfloat16)
        .reshape(seq_count, tok_count, width)
    )
    all_keys, all_values, all_ids = (
        lax.all_gather(key_rows, "seq", axis=1, tiled=True),
        lax.all_gather(value_rows, "seq", axis=1, tiled=True),
        lax.all_gather(local_ids, "seq", axis=1, tiled=True),
    )
    attn_mixed, log_total = attend_forward(
        query_rows, all_keys, all_values, local_ids, all_ids, heads
    )
    mixed_low = attn_mixed.reshape(-1, width).astype(jnp.bfloat16)
    branch = matmul(mixed_low, w_out) + b_out
    hidden_one = flat_rows.astype(jnp.float32) + branch
    normed, norm_one_pull = jax.vjp(layer_norm, hidden_one, gain_attn, shift_attn)
    normed_low = normed.astype(jnp.bfloat16)
    up_pre = matmul(normed_low, w_up) + b_up
    active, gelu_pull = jax.vjp(exact_gelu, up_pre)
    active_low = active.astype(jnp.bfloat16)
    down_out = matmul(active_low, w_down) + b_down
    result, norm_two_pull = jax.vjp(layer_norm, normed + down_out, gain_out, shift_out)
    member = (local_ids[:, :, None] == lax.iota(jnp.int32, SEGS)[None, None, :]).astype(jnp.float32)
    seg_sums = jnp.einsum(
        "ntg,ntd->ngd", member, result.reshape(seq_count, tok_count, width), precision=highest
    )
    seg_sums = lax.psum(seg_sums, "seq")
    pooled, pool_pull = jax.vjp(pool_finish, seg_sums)
    (grad_sums,) = pool_pull(local_pool_cot)
    grad_result = local_cot.astype(jnp.float32) + jnp.einsum(
        "ntg,ngd->ntd", member, grad_sums, precision=highest
    )
    grad_hidden_two, grad_gain_out, grad_shift_out = norm_two_pull(grad_result.reshape(-1, width))
    grad_down = grad_hidden_two.astype(jnp.bfloat16)
    grad_b_down = jnp.sum(grad_down.astype(jnp.float32), axis=0)
    grad_w_down = transpose_dot(active_low, grad_down)
    (grad_up,) = gelu_pull(back_dot(grad_down, w_down))
    grad_up_low = grad_up.astype(jnp.bfloat16)
    grad_b_up = jnp.sum(grad_up_low.astype(jnp.float32), axis=0)
    grad_w_up = transpose_dot(normed_low, grad_up_low)
    grad_normed = grad_hidden_two + back_dot(grad_up_low, w_up)
    grad_hidden_one, grad_gain_attn, grad_shift_attn = norm_one_pull(grad_normed)
    grad_branch = grad_hidden_one.astype(jnp.bfloat16)
    grad_b_out = jnp.sum(grad_branch.astype(jnp.float32), axis=0)
    grad_w_out = transpose_dot(mixed_low, grad_branch)
    grad_mixed = (
        back_dot(grad_branch, w_out).astype(jnp.bfloat16).reshape(seq_count, tok_count, width)
    )
    grad_query, keys_part, values_part = attend_backward(
        query_rows, all_keys, all_values, local_ids, all_ids, log_total, grad_mixed, heads
    )
    grad_keys, grad_values = (
        lax.psum_scatter(
            keys_part.astype(jnp.bfloat16), "seq", scatter_dimension=1, tiled=True
        ).astype(jnp.float32),
        lax.psum_scatter(
            values_part.astype(jnp.bfloat16), "seq", scatter_dimension=1, tiled=True
        ).astype(jnp.float32),
    )
    query_low = grad_query.reshape(-1, width).astype(jnp.bfloat16)
    keys_low = grad_keys.reshape(-1, width).astype(jnp.bfloat16)
    values_low = grad_values.reshape(-1, width).astype(jnp.bfloat16)
    grad_w_query = transpose_dot(flat_rows, query_low)
    grad_w_key = transpose_dot(flat_rows, keys_low)
    grad_w_value = transpose_dot(flat_rows, values_low)
    grad_b_query = jnp.sum(query_low.astype(jnp.float32), axis=0)
    grad_b_value = jnp.sum(values_low.astype(jnp.float32), axis=0)
    grad_input = (
        grad_hidden_one
        + back_dot(query_low, w_query)
        + back_dot(keys_low, w_key)
        + back_dot(values_low, w_value)
    )
    layer_out = result.astype(jnp.bfloat16).reshape(seq_count, tok_count, width)
    grad_tokens = grad_input.astype(jnp.bfloat16).reshape(seq_count, tok_count, width)
    shares = (
        lax.psum_scatter(grad_w_query, "rows", scatter_dimension=0, tiled=True),
        lax.psum_scatter(grad_w_key, "rows", scatter_dimension=0, tiled=True),
        lax.psum_scatter(grad_w_value, "rows", scatter_dimension=0, tiled=True),
        lax.psum_scatter(grad_b_query, "rows", scatter_dimension=0, tiled=True),
        lax.psum_scatter(grad_b_value, "rows", scatter_dimension=0, tiled=True),
        lax.psum_scatter(grad_w_out, "rows", scatter_dimension=0, tiled=True),
        lax.psum_scatter(grad_b_out, "rows", scatter_dimension=0, tiled=True),
        lax.psum_scatter(grad_gain_attn, "rows", scatter_dimension=0, tiled=True),
        lax.psum_scatter(grad_shift_attn, "rows", scatter_dimension=0, tiled=True),
        lax.psum_scatter(grad_w_up, "rows", scatter_dimension=0, tiled=True),
        lax.psum_scatter(grad_b_up, "rows", scatter_dimension=0, tiled=True),
        lax.psum_scatter(grad_w_down, "rows", scatter_dimension=0, tiled=True),
        lax.psum_scatter(grad_b_down, "rows", scatter_dimension=0, tiled=True),
        lax.psum_scatter(grad_gain_out, "rows", scatter_dimension=0, tiled=True),
        lax.psum_scatter(grad_shift_out, "rows", scatter_dimension=0, tiled=True),
    )
    totals = (
        lax.psum(shares[0].astype(jnp.bfloat16), "seq").astype(jnp.float32),
        lax.psum(shares[1].astype(jnp.bfloat16), "seq").astype(jnp.float32),
        lax.psum(shares[2].astype(jnp.bfloat16), "seq").astype(jnp.float32),
        lax.psum(shares[3].astype(jnp.bfloat16), "seq").astype(jnp.float32),
        lax.psum(shares[4].astype(jnp.bfloat16), "seq").astype(jnp.float32),
        lax.psum(shares[5].astype(jnp.bfloat16), "seq").astype(jnp.float32),
        lax.psum(shares[6].astype(jnp.bfloat16), "seq").astype(jnp.float32),
        lax.psum(shares[7].astype(jnp.bfloat16), "seq").astype(jnp.float32),
        lax.psum(shares[8].astype(jnp.bfloat16), "seq").astype(jnp.float32),
        lax.psum(shares[9].astype(jnp.bfloat16), "seq").astype(jnp.float32),
        lax.psum(shares[10].astype(jnp.bfloat16), "seq").astype(jnp.float32),
        lax.psum(shares[11].astype(jnp.bfloat16), "seq").astype(jnp.float32),
        lax.psum(shares[12].astype(jnp.bfloat16), "seq").astype(jnp.float32),
        lax.psum(shares[13].astype(jnp.bfloat16), "seq").astype(jnp.float32),
        lax.psum(shares[14].astype(jnp.bfloat16), "seq").astype(jnp.float32),
    )
    return (
        layer_out,
        pooled,
        grad_tokens,
        totals[0],
        totals[1],
        totals[2],
        totals[3],
        totals[4],
        totals[5],
        totals[6],
        totals[7],
        totals[8],
        totals[9],
        totals[10],
        totals[11],
        totals[12],
        totals[13],
        totals[14],
    )


def solution(mesh):
    in_specs = (
        P("rows", "seq", None),
        P("rows", "seq"),
        P(),
        P(),
        P(),
        P(),
        P(),
        P(),
        P(),
        P(),
        P(),
        P(),
        P(),
        P(),
        P(),
        P(),
        P(),
        P("rows", "seq", None),
        P("rows", None, None),
    )
    out_specs = (
        P("rows", "seq", None),
        P("rows", None, None),
        P("rows", "seq", None),
        P("rows", None),
        P("rows", None),
        P("rows", None),
        P("rows"),
        P("rows"),
        P("rows", None),
        P("rows"),
        P("rows"),
        P("rows"),
        P("rows", None),
        P("rows"),
        P("rows", None),
        P("rows"),
        P("rows"),
        P("rows"),
    )
    return jax.shard_map(local, mesh=mesh, in_specs=in_specs, out_specs=out_specs, check_vma=False)
```

profile of v0, /device:TPU:0, one launch (start us, length us, event | category | flops | bytes accessed | tf_op | source)
XLA Modules:
  0.0 992.7 jit_solution(5668774894956338449)
XLA Ops:
  15.0 6.5 all_gather.10
  21.7 20.3 %all-gather.5.cloned.1.call-done = bf16[4,512,768]{2,1,0:T(8,128)(2,1)} async-done(((bf16[4,128,768]{2,1,0:T(8,128)(2,1)}), bf16[4,512,768]{2,1,0:T(8,128)(2,1)}) %all-gather.5.cloned.1.call-update) | async-done | bytes 3145744 | tf_op jit(solution)/shard_map/all_gather | solution.py:165
  42.0 4.7 copy.65
  46.7 4.0 fusion.12
  50.7 4.8 copy-done.1
  55.6 3.7 fusion
  59.3 13.4 %all-gather.3.cloned.1.call-done = bf16[4,512,768]{2,1,0:T(8,128)(2,1)} async-done(((bf16[4,128,768]{2,1,0:T(8,128)(2,1)}), bf16[4,512,768]{2,1,0:T(8,128)(2,1)}) %all-gather.3.cloned.1.call-update) | async-done | bytes 3145744 | tf_op jit(solution)/shard_map/all_gather | solution.py:166
  72.7 4.7 copy.63
  77.4 7.7 fusion.19
  87.2 29.3 %multiply_convert_fusion.2 = (bf16[512,3072]{1,0:T(8,128)(2,1)S(1)}, f32[512,3072]{1,0:T(8,128)}, f32[512,3072]{1,0:T(8,128)}) fusion(f32[3072]{0:T(1024)S(1)} %copy-done.29, bf16[768,3072]{1,0:T(8,128)(2,1)S(1)} %bitcast.129, f32[512,768]{1,0:T(8,128)S(1)} %get-tuple-element.146, f32[768]{0:T(1024)S(1)} %copy-done.34, f32[768]{0:T(1024)S(1)} %copy-done.28, ...), kind=kOutput, calls=%fused_computation.15 | convolution fusion | flops 2521694208 | bytes 22042624 | tf_op jit(solution)/shard_map/dot_general | solution.py:16
  122.4 31.4 %all-reduce.19.cloned.1.call-done = f32[4,8,768]{2,1,0:T(8,128)} async-done(((f32[4,8,768]{2,1,0:T(8,128)}), f32[4,8,768]{2,1,0:T(8,128)}) %all-reduce.19.cloned.1.call-update) | async-done | bytes 98320 | tf_op jit(solution)/shard_map/psum | solution.py:186
  168.6 9.5 convert_reduce_fusion
  178.1 3.7 multiply_reduce_fusion.1
  190.6 9.5 fusion.13
  200.2 4.7 copy.74
  204.9 9.3 multiply_reduce_fusion
  214.3 7.2 multiply_convert_fusion
  225.1 4.7 copy.72
  234.3 6.1 convert_reduce_fusion.4
  246.5 3.6 convolution_bitcast_fusion
  253.6 29.8 %reduce-scatter.15.cloned.1.call-done = bf16[4,128,768]{2,1,0:T(8,128)(2,1)} async-done(((bf16[4,512,768]{2,1,0:T(8,128)(2,1)}), bf16[4,128,768]{2,1,0:T(8,128)(2,1)}) %reduce-scatter.15.cloned.1.call-update) | async-done | bytes 786448 | tf_op jit(solution)/shard_map/reduce_scatter | solution.py:212
  283.4 3.6 convolution_bitcast_fusion.1
  290.3 8.9 fusion.65
  299.3 8.4 fusion.77
  314.1 42.1 %reduce-scatter.19.cloned.1.call-done = f32[96,768]{1,0:T(8,128)} async-done(((f32[768,768]{1,0:T(8,128)}), f32[96,768]{1,0:T(8,128)}) %reduce-scatter.19.cloned.1.call-update) | async-done | bytes 294928 | tf_op jit(solution)/shard_map/reduce_scatter | solution.py:241
  357.9 70.3 %reduce-scatter.25.cloned.1.call-done = f32[96,768]{1,0:T(8,128)} async-done(((f32[768,768]{1,0:T(8,128)}), f32[96,768]{1,0:T(8,128)}) %reduce-scatter.25.cloned.1.call-update) | async-done | bytes 294928
  430.0 70.2 %reduce-scatter.29.cloned.1.call-done = f32[96,768]{1,0:T(8,128)} async-done(((f32[768,768]{1,0:T(8,128)}), f32[96,768]{1,0:T(8,128)}) %reduce-scatter.29.cloned.1.call-update) | async-done | bytes 294928
  502.0 70.2 %reduce-scatter.27.cloned.1.call-done = f32[96,768]{1,0:T(8,128)} async-done(((f32[768,768]{1,0:T(8,128)}), f32[96,768]{1,0:T(8,128)}) %reduce-scatter.27.cloned.1.call-update) | async-done | bytes 294928
  573.9 164.7 %reduce-scatter.21.cloned.1.call-done = f32[96,3072]{1,0:T(8,128)} async-done(((f32[768,3072]{1,0:T(8,128)}), f32[96,3072]{1,0:T(8,128)}) %reduce-scatter.21.cloned.1.call-update) | async-done | bytes 1179664 | tf_op jit(solution)/shard_map/reduce_scatter | solution.py:245
  740.8 164.5 %reduce-scatter.23.cloned.1.call-done = f32[384,768]{1,0:T(8,128)} async-done(((f32[3072,768]{1,0:T(8,128)}), f32[384,768]{1,0:T(8,128)}) %reduce-scatter.23.cloned.1.call-update) | async-done | bytes 1179664 | tf_op jit(solution)/shard_map/reduce_scatter | solution.py:247
  908.2 36.3 %all-reduce.13 = (bf16[768]{0:T(1024)(128)(2,1)}, bf16[768]{0:T(1024)(128)(2,1)}, bf16[768]{0:T(1024)(128)(2,1)}, bf16[768]{0:T(1024)(128)(2,1)}, bf16[768]{0:T(...) all-reduce(f32[768]{0:T(1024)} %reduce_sum.336, ...), channel_id=7, replica_groups=mesh['rows'=8,'seq'=4] {'rows'}, use_global_device_ids=true, to_apply=%region_31.32.clone | all-reduce | flops 9216 | bytes 55296
  954.8 6.5 all-reduce.14
  (205 shorter events, 112.0 us)
Async XLA Ops:
  7.2 78.6 %copy-start = (bf16[768,768]{1,0:T(8,128)(2,1)S(1)}, bf16[768,768]{1,0:T(8,128)(2,1)}, u32[]{:S(2)}) copy-start(bf16[768,768]{1,0:T(8,128)(2,1)} %param.26) | copy-start | bytes 3538948
  7.2 34.8 %all-gather.5.cloned.1.call-start = ((), (), s32[]{:S(2)}) async-start(), calls=%async_computation.9 | async-start | bytes 3932160 | tf_op jit(solution)/shard_map/all_gather | solution.py:165
  10.6 62.1 %all-gather.3.cloned.1.call-start = ((), (), s32[]{:S(2)}) async-start(), calls=%async_computation.8 | async-start | bytes 3932160 | tf_op jit(solution)/shard_map/all_gather | solution.py:166
  12.4 141.3 %all-reduce.19.cloned.1.call-start = ((), (), s32[]{:S(2)}) async-start(), calls=%async_computation.10 | async-start | bytes 196608 | tf_op jit(solution)/shard_map/psum | solution.py:186
  15.0 31.7 %copy-start.3 = (bf16[4,128,12,64]{1,0,3,2:T(4,128)(2,1)}, bf16[4,128,12,64]{1,0,3,2:T(4,128)(2,1)S(1)}, u32[]{:S(2)}) copy-start(bf16[4,128,12,64]{1,0,3,2:T(4,128)(2,1)S(1)} %reshape_reshape.4) | copy-start | bytes 2359300
  72.7 14.4 %slice-start.2 = ((s8[4718592]{0:T(1024)(128)(4,1)}), s8[524288]{0:T(1024)(128)(4,1)S(1)}, s32[]{:S(2)}) async-start(s8[4718592]{0:T(1024)(128)(4,1)} %bitcast.128), calls=%async_computation.22 | async-start | bytes 1048576
  77.4 9.7 slice-start.3
  85.8 30.7 %slice-start = ((s8[4718592]{0:T(1024)(128)(4,1)}), s8[4194304]{0:T(1024)(128)(4,1)S(1)}, s32[]{:S(2)}) async-start(s8[4718592]{0:T(1024)(128)(4,1)} %bitcast.126), calls=%async_computation.20 | async-start | bytes 8388608
  86.8 29.8 %copy-start.5 = (f32[512,768]{1,0:T(8,128)}, f32[512,768]{1,0:T(8,128)S(1)}, u32[]{:S(2)}) copy-start(f32[512,768]{1,0:T(8,128)S(1)} %get-tuple-element.146) | copy-start | bytes 4718596
  87.2 94.6 %copy-start.26 = (f32[512]{0:T(512)}, f32[512]{0:T(512)S(1)}, u32[]{:S(2)}) copy-start(f32[512]{0:T(512)S(1)} %fusion.53) | copy-start | bytes 6148
  87.2 29.4 %slice-start.1 = ((s8[4718592]{0:T(1024)(128)(4,1)}), s8[524288]{0:T(1024)(128)(4,1)S(1)}, s32[]{:S(2)}) async-start(s8[4718592]{0:T(1024)(128)(4,1)} %bitcast.126), calls=%async_computation.21 | async-start | bytes 1048576
  87.2 29.4 %copy-start.33 = (f32[768]{0:T(1024)S(1)}, f32[768]{0:T(1024)}, u32[]{:S(2)}) copy-start(f32[768]{0:T(1024)} %param.33) | copy-start | bytes 9220
  119.7 34.0 %copy-start.14 = (f32[4,8,1728]{2,1,0:T(8,128)S(1)}, f32[4,8,1728]{2,1,0:T(8,128)}, u32[]{:S(2)}) copy-start(f32[4,8,1728]{2,1,0:T(8,128)} %param.37) | copy-start | bytes 663556
  122.3 124.2 %reduce-scatter.17.cloned.1.call-start = ((), (), s32[]{:S(2)}) async-start(), calls=%async_computation.12 | async-start | bytes 3932160 | tf_op jit(solution)/shard_map/reduce_scatter | solution.py:215
  167.1 11.0 %slice-start.4 = ((s8[4718592]{0:T(1024)(128)(4,1)}), s8[4194304]{0:T(1024)(128)(4,1)S(1)}, s32[]{:S(2)}) async-start(s8[4718592]{0:T(1024)(128)(4,1)} %bitcast.130), calls=%async_computation.24 | async-start | bytes 8388608
  168.6 9.5 copy-start.15
  168.6 9.5 copy-start.6
  168.6 9.5 slice-start.5
  204.9 78.5 %reduce-scatter.15.cloned.1.call-start = ((), (), s32[]{:S(2)}) async-start(), calls=%async_computation.11 | async-start | bytes 3932160 | tf_op jit(solution)/shard_map/reduce_scatter | solution.py:212
  229.8 126.4 %reduce-scatter.19.cloned.1.call-start = ((), (), s32[]{:S(2)}) async-start(), calls=%async_computation.13 | async-start | bytes 2654208 | tf_op jit(solution)/shard_map/reduce_scatter | solution.py:241
  234.3 193.9 %reduce-scatter.25.cloned.1.call-start = ((), (), s32[]{:S(2)}) async-start(), calls=%async_computation.16 | async-start | bytes 2654208
  246.4 253.8 %reduce-scatter.29.cloned.1.call-start = ((), (), s32[]{:S(2)}) async-start(), calls=%async_computation.18 | async-start | bytes 2654208
  253.6 318.6 %reduce-scatter.27.cloned.1.call-start = ((), (), s32[]{:S(2)}) async-start(), calls=%async_computation.17 | async-start | bytes 2654208
  290.1 448.6 %reduce-scatter.21.cloned.1.call-start = ((), (), s32[]{:S(2)}) async-start(), calls=%async_computation.14 | async-start | bytes 10616832 | tf_op jit(solution)/shard_map/reduce_scatter | solution.py:245
  299.2 606.1 %reduce-scatter.23.cloned.1.call-start = ((), (), s32[]{:S(2)}) async-start(), calls=%async_computation.15 | async-start | bytes 10616832 | tf_op jit(solution)/shard_map/reduce_scatter | solution.py:247
  307.7 667.7 %all-reduce.21.cloned.1.call-start = ((), (), s32[]{:S(2)}) async-start(), calls=%async_computation.19 | async-start | bytes 3833856 | tf_op jit(solution)/shard_map/psum | solution.py:253
  430.0 477.5 %copy-start.7 = (bf16[4,128,768]{2,1,0:T(8,128)(2,1)S(1)}, bf16[4,128,768]{2,1,0:T(8,128)(2,1)}, u32[]{:S(2)}) copy-start(bf16[4,128,768]{2,1,0:T(8,128)(2,1)} %reduce-scatter.17.cloned.1.call-done) | copy-start | bytes 2359300
  573.9 334.3 %copy-start.23 = (f32[768]{0:T(1024)S(1)}, f32[768]{0:T(1024)}, u32[]{:S(2)}) copy-start(f32[768]{0:T(1024)} %get-tuple-element.155) | copy-start | bytes 9220
  573.9 334.3 %copy-start.24 = (f32[768]{0:T(1024)S(1)}, f32[768]{0:T(1024)}, u32[]{:S(2)}) copy-start(f32[768]{0:T(1024)} %get-tuple-element.72) | copy-start | bytes 9220
  573.9 334.3 %copy-start.25 = (f32[768]{0:T(1024)S(1)}, f32[768]{0:T(1024)}, u32[]{:S(2)}) copy-start(f32[768]{0:T(1024)} %get-tuple-element.111) | copy-start | bytes 9220
  961.3 12.3 %copy-start.11 = (f32[512,768]{1,0:T(8,128)S(1)}, f32[512,768]{1,0:T(8,128)}, u32[]{:S(2)}) copy-start(f32[512,768]{1,0:T(8,128)} %fusion.22) | copy-start | bytes 4718596
  961.3 12.3 %copy-start.13 = (bf16[768,768]{1,0:T(8,128)(2,1)S(1)}, bf16[768,768]{1,0:T(8,128)(2,1)}, u32[]{:S(2)}) copy-start(bf16[768,768]{1,0:T(8,128)(2,1)} %param.23) | copy-start | bytes 3538948
  (24 other events, 84.6 us)
Sparse Core Ops, SparseCore 0:
  10.8 31.2 all-gather.4
  44.1 28.5 all-gather.2
  122.4 31.2 all-reduce.18
  205.0 37.9 reduce-scatter.16
  245.4 37.9 reduce-scatter.14
  287.2 69.0 reduce-scatter.18
  360.1 68.0 reduce-scatter.24
  432.1 68.0 reduce-scatter.28
  504.1 68.0 reduce-scatter.26
  576.0 162.5 reduce-scatter.20
  742.6 162.5 reduce-scatter.22
  909.3 48.6 all-reduce.20
where the time goes:
time: 992 us; the launch traced here: 993 us
  waiting for transfers between devices  677 us (68%)
  matrix products  136 us (14%)
  local copies, waits for them, and re-layouts  66 us (7%)
  blocking collectives  49.3 us (5%)
  other arithmetic  47.3 us (5%)
  between operations  16.4 us (2%)
    unnamed x15, waiting for transfers between devices  211 us
    reduce_scatter x1, waiting for transfers between devices, local(): lax.psum_scatter(grad_w_up, 'rows', scatter_dimension=0, tiled=True)  165 us
    reduce_scatter x1, waiting for transfers between devices, local(): lax.psum_scatter(grad_w_down, 'rows', scatter_dimension=0, tiled=True)  165 us
    reduce_scatter x1, waiting for transfers between devices, local(): lax.psum_scatter(grad_w_out, 'rows', scatter_dimension=0, tiled=True)  42.1 us
    dot_general x6, matrix products, matmul(): return jnp.dot(left, right, preferred_element_type=jnp.float32)  40.1 us
    unnamed x107, local copies, waits for them, and re-layouts  40.1 us
    unnamed x1, blocking collectives  36.3 us
    psum x1, waiting for transfers between devices, local(): seg_sums = lax.psum(seg_sums, 'seq')  31.4 us
  transfers between devices with their start and end apart: 12, of which 10 were waited for; matrix products, arithmetic and copies ran while one was open for 13% of the time, Pallas kernels for 0%

commit v1 on v0

v1 whole, which is shorter than its diff:
```python
import functools

import jax
import jax.numpy as jnp
from jax import lax
from jax.experimental import pallas as pl
from jax.experimental.pallas import tpu as pltpu
from jax.sharding import PartitionSpec as P

HEADS = 12
SEGS = 8
norm_eps = 1e-12
pool_eps = 1e-06
bf16 = jnp.bfloat16
f32 = jnp.float32
MIB = 2**20


def shape(dims, dtype=bf16):
    return jax.ShapeDtypeStruct(dims, dtype)


def dot(left, right, left_dim=1, right_dim=0):
    return lax.dot_general(
        left, right, (((left_dim,), (right_dim,)), ((), ())), preferred_element_type=f32
    )


def whole(dims):
    zeros = (0,) * len(dims)
    return pl.BlockSpec(dims, lambda *_: zeros, pipeline_mode=pl.Buffered(1))


def whole_out(dims):
    zeros = (0,) * len(dims)
    return pl.BlockSpec(dims, lambda *_: zeros)


def params(mib):
    return pltpu.CompilerParams(vmem_limit_bytes=mib * MIB)


def split_two(value):
    high = value.astype(bf16)
    return high, (value - high.astype(f32)).astype(bf16)


def split_three(value):
    high = value.astype(bf16)
    rest = value - high.astype(f32)
    mid, low = split_two(rest)
    return high, mid, low


def attend_kernel(
    t0, t1, t2, t3, wq, wk, wv, wo, bq, bv, bo, gain, shift,
    exp_out, total_out, row_out, q_out, k_out, v_out, mix_t, mixed_out, norm_out, rstd_out, low_out, ids_out,
    mask,
):
    step = pl.program_id(0)
    blocks = (t0, t1, t2, t3)
    part = t0.shape[0] - 16
    length = part * 4

    @pl.when(step == 0)
    def _():
        for at, block in enumerate(blocks):
            row_out[at * part : (at + 1) * part, :] = block[:part, :]
        rows = row_out[...]
        q_out[...] = (dot(rows, wq[...]) + bq[...]).astype(bf16) * bf16(0.125)
        k_out[...] = dot(rows, wk[...]).astype(bf16)
        v_out[...] = (dot(rows, wv[...]) + bv[...]).astype(bf16)
        ids = jnp.concatenate([block[part : part + 16, :part].astype(f32)[0:1] for block in blocks], axis=1)
        ids_out[...] = jnp.broadcast_to(ids, ids_out.shape)
        column = jnp.broadcast_to(ids, (128, length)).T[:, 0:1]
        mask[...] = jnp.where(column == ids, 0.0, -1e30)

    lanes = pl.ds(pl.multiple_of(step * 128, 128), 128)
    keys = k_out[:, lanes]
    query_t = q_out[:, lanes].T
    value_t = v_out[:, lanes].T
    for half in range(2):
        at = slice(half * 64, half * 64 + 64)
        scores = dot(keys[:, at], query_t[at, :]) + mask[...]
        expo = jnp.exp(scores - jnp.max(scores, axis=0, keepdims=True))
        inverse = 1.0 / jnp.sum(expo, axis=0, keepdims=True)
        low = expo.astype(bf16)
        exp_out[half] = low
        total_out[0, half : half + 1, :] = inverse
        mix_t[pl.ds(pl.multiple_of(step * 128 + half * 64, 64), 64), :] = dot(value_t[at, :], low) * inverse

    @pl.when(step == pl.num_programs(0) - 1)
    def _():
        mixed = mix_t[...].astype(bf16).T
        mixed_out[...] = mixed
        hidden = row_out[...].astype(f32) + (dot(mixed, wo[...]) + bo[...])
        centered = hidden - jnp.mean(hidden, axis=-1, keepdims=True)
        rstd = lax.rsqrt(jnp.mean(centered * centered, axis=-1, keepdims=True) + norm_eps)
        normal = centered * rstd
        norm_out[...] = normal
        rstd_out[...] = jnp.broadcast_to(rstd, rstd_out.shape)
        low_out[...] = (normal * gain[...] + shift[...]).astype(bf16)


def attend(blocks, wq, wk, wv, wo, bq, bv, bo, gain, shift):
    part, width = blocks[0].shape
    length = (part - 16) * 4
    pairs = width // 128
    square = whole((width, width))
    vec = whole((1, width))
    flat = whole_out((length, width))
    return pl.pallas_call(
        attend_kernel,
        grid=(pairs,),
        in_specs=[whole((part, width))] * 4 + [square] * 4 + [vec] * 5,
        out_specs=[
            pl.BlockSpec((2, length, length), lambda i: (i, 0, 0)),
            pl.BlockSpec((1, 8, length), lambda i: (i, 0, 0)),
            flat, flat, flat, flat,
            whole_out((width, length)),
            flat, flat,
            whole_out((length, 128)),
            flat,
            whole_out((8, length)),
        ],
        out_shape=[
            shape((2 * pairs, length, length)),
            shape((pairs, 8, length), f32),
            shape((length, width)),
            shape((length, width)),
            shape((length, width)),
            shape((length, width)),
            shape((width, length), f32),
            shape((length, width)),
            shape((length, width), f32),
            shape((length, 128), f32),
            shape((length, width)),
            shape((8, length), f32),
        ],
        scratch_shapes=[pltpu.VMEM((length, length), f32)],
        compiler_params=params(56),
        name="attend_forward",
    )(*blocks, wq, wk, wv, wo, bq, bv, bo, gain, shift)


def gelu_both(v):
    bell = jnp.exp(v * v * -0.5)
    t = 1.0 / (1.0 + (0.3275911 * 0.7071067811865476) * jnp.abs(v))
    poly = ((((1.061405429 * t - 1.453152027) * t + 1.421413741) * t - 0.284496736) * t + 0.254829592) * t
    tail = 0.5 * poly * bell
    phi = jnp.where(v < 0, tail, 1.0 - tail)
    return v * phi, phi + v * bell * 0.3989422804014327


def pool_windows(width):
    return (width, width * 2 // 3, width // 3, width // 6, width // 12)


def feed_kernel(
    core, low, w_up, b_up, w_down, normal, gain_a, shift_a, b_down, gain, shift, c0, c1, c2, c3, ids, pool_cot,
    act_out, slope_out, l0, l1, l2, l3, pooled_out, hidden_out, keep_out, send_out, low_out, sums_out,
    acc,
):
    step = pl.program_id(0)
    length, width = low.shape
    up = dot(low[...], w_up[...]) + b_up[...]
    active, slope = gelu_both(up)
    active_low = active.astype(bf16)
    act_out[...] = active_low
    slope_out[...] = slope.astype(bf16)
    down = dot(active_low, w_down[...])

    @pl.when(step == 0)
    def _():
        acc[...] = down

    @pl.when(step > 0)
    def _():
        acc[...] += down

    @pl.when(step == pl.num_programs(0) - 1)
    def _():
        part = length // 4
        hidden = normal[...] * gain_a[...] + shift_a[...] + (acc[...] + b_down[...])
        centered = hidden - jnp.mean(hidden, axis=-1, keepdims=True)
        rstd = lax.rsqrt(jnp.mean(centered * centered, axis=-1, keepdims=True) + norm_eps)
        unit = centered * rstd
        result = unit * gain[...] + shift[...]
        for at, out in enumerate((l0, l1, l2, l3)):
            out[...] = result[at * part : (at + 1) * part].astype(bf16)
        groups = lax.broadcasted_iota(jnp.int32, (16, length), 0).astype(f32)
        member = jnp.where((groups == ids[0:1, :]) & (groups < SEGS), 1.0, 0.0).astype(bf16)
        seg_sums = sum(dot(member, piece) for piece in split_three(result))[:SEGS]
        at = 0
        grad_sums = []
        for window in pool_windows(width):
            sums = seg_sums[:, :window]
            cot = pool_cot[:, at : at + window]
            factor = lax.rsqrt(jnp.mean(sums * sums, axis=-1, keepdims=True) + pool_eps)
            pooled_out[:, at : at + window] = sums * factor
            inner = jnp.sum(cot * sums, axis=-1, keepdims=True) * (factor * factor * factor / window)
            piece = cot * factor - sums * inner
            if window < width:
                piece = jnp.concatenate([piece, jnp.zeros((SEGS, width - window), f32)], axis=1)
            grad_sums.append(piece)
            at += window
        total = jnp.concatenate([sum(grad_sums), jnp.zeros((16 - SEGS, width), f32)], axis=0)
        spread = sum(dot(member, piece, 0, 0) for piece in split_two(total))
        cot = jnp.concatenate([c[...].astype(f32) for c in (c0, c1, c2, c3)], axis=0)
        grad = cot + spread
        scaled = grad * gain[...]
        hidden_grad = rstd * (
            scaled
            - jnp.mean(scaled, axis=-1, keepdims=True)
            - unit * jnp.mean(scaled * unit, axis=-1, keepdims=True)
        )
        hidden_out[...] = hidden_grad
        rounded = hidden_grad.astype(bf16)
        low_out[...] = rounded
        half = width // 2
        first = core[0] == 0
        keep_out[...] = jnp.where(first, rounded[:, :half], rounded[:, half:])
        send_out[...] = jnp.where(first, rounded[:, half:], rounded[:, :half])
        sums_out[...] = jnp.concatenate(
            [
                jnp.sum(grad * unit, axis=0, keepdims=True),
                jnp.sum(grad, axis=0, keepdims=True),
                jnp.sum(rounded.astype(f32), axis=0, keepdims=True),
                jnp.zeros((5, width), f32),
            ],
            axis=0,
        )


def feed(core, low, w_up, b_up, w_down, normal, gain_a, shift_a, b_down, gain, shift, cots, ids, pool_cot):
    length, width = low.shape
    hidden = w_up.shape[1]
    tile = 512
    part = length // 4
    vec = whole((1, width))
    flat = whole_out((length, width))
    halves = whole_out((length, width // 2))
    return pl.pallas_call(
        feed_kernel,
        grid=(hidden // tile,),
        in_specs=[
            pl.BlockSpec(memory_space=pltpu.SMEM),
            whole((length, width)),
            pl.BlockSpec((width, tile), lambda i: (0, i)),
            pl.BlockSpec((1, tile), lambda i: (0, i)),
            pl.BlockSpec((tile, width), lambda i: (i, 0)),
            whole((length, width)),
            vec, vec, vec, vec, vec,
            *[whole((part, width))] * 4,
            whole((8, length)),
            whole(pool_cot.shape),
        ],
        out_specs=[
            pl.BlockSpec((length, tile), lambda i: (0, i)),
            pl.BlockSpec((length, tile), lambda i: (0, i)),
            *[whole_out((part, width))] * 4,
            whole_out(pool_cot.shape),
            flat, halves, halves, flat,
            whole_out((8, width)),
        ],
        out_shape=[
            shape((length, hidden)),
            shape((length, hidden)),
            *[shape((part, width))] * 4,
            shape(pool_cot.shape, f32),
            shape((length, width), f32),
            shape((length, width // 2)),
            shape((length, width // 2)),
            shape((length, width)),
            shape((8, width), f32),
        ],
        scratch_shapes=[pltpu.VMEM((length, width), f32)],
        compiler_params=params(56),
        name="feed_forward",
    )(core, low, w_up, b_up, w_down, normal, gain_a, shift_a, b_down, gain, shift, *cots, ids, pool_cot)


def feed_back_kernel(
    core, grad_low, w_down, slope, w_up, hidden, normal, rstd, gain, wo,
    keep_out, send_out, b_up_out, hidden_out, mixed_out, keep_b, send_b, sums_out,
    acc,
):
    step = pl.program_id(0)
    steps = pl.num_programs(0)
    width = hidden.shape[1]
    grad_up = (dot(grad_low[...], w_down[...], 1, 1) * slope[...].astype(f32)).astype(bf16)
    kept = (step // (steps // 2)) == core[0]

    @pl.when(kept)
    def _():
        keep_out[...] = grad_up

    @pl.when(jnp.logical_not(kept))
    def _():
        send_out[...] = grad_up

    b_up_out[...] = jnp.broadcast_to(jnp.sum(grad_up.astype(f32), axis=0, keepdims=True), b_up_out.shape)
    back = dot(grad_up, w_up[...], 1, 1)

    @pl.when(step == 0)
    def _():
        acc[...] = back

    @pl.when(step > 0)
    def _():
        acc[...] += back

    @pl.when(step == steps - 1)
    def _():
        grad = hidden[...] + acc[...]
        unit = normal[...]
        scaled = grad * gain[...]
        hidden_grad = rstd[:, 0:1] * (
            scaled
            - jnp.mean(scaled, axis=-1, keepdims=True)
            - unit * jnp.mean(scaled * unit, axis=-1, keepdims=True)
        )
        hidden_out[...] = hidden_grad
        rounded = hidden_grad.astype(bf16)
        mixed_out[...] = dot(rounded, wo[...], 1, 1).astype(bf16)
        half = width // 2
        first = core[0] == 0
        keep_b[...] = jnp.where(first, rounded[:, :half], rounded[:, half:])
        send_b[...] = jnp.where(first, rounded[:, half:], rounded[:, :half])
        sums_out[...] = jnp.concatenate(
            [
                jnp.sum(grad * unit, axis=0, keepdims=True),
                jnp.sum(grad, axis=0, keepdims=True),
                jnp.sum(rounded.astype(f32), axis=0, keepdims=True),
                jnp.zeros((5, width), f32),
            ],
            axis=0,
        )


def feed_back(core, grad_low, w_down, slope, w_up, hidden, normal, rstd, gain, wo):
    length, width = grad_low.shape
    feed_width = w_up.shape[1]
    tile = 512
    steps = feed_width // tile
    per = steps // 2
    flat = whole((length, width))
    halves = whole_out((length, width // 2))
    return pl.pallas_call(
        feed_back_kernel,
        grid_spec=pltpu.PrefetchScalarGridSpec(
            num_scalar_prefetch=1,
            grid=(steps,),
            in_specs=[
                flat,
                pl.BlockSpec((tile, width), lambda i, c: (i, 0)),
                pl.BlockSpec((length, tile), lambda i, c: (0, i)),
                pl.BlockSpec((width, tile), lambda i, c: (0, i)),
                flat,
                flat,
                whole((length, 128)),
                whole((1, width)),
                whole((width, width)),
            ],
            out_specs=[
                pl.BlockSpec((length, tile), lambda i, c: (0, jnp.clip(i - per * c[0], 0, per - 1))),
                pl.BlockSpec((length, tile), lambda i, c: (0, jnp.clip(i - per * (1 - c[0]), 0, per - 1))),
                pl.BlockSpec((8, tile), lambda i, c: (0, i)),
                whole_out((length, width)),
                whole_out((length, width)),
                halves,
                halves,
                whole_out((8, width)),
            ],
            scratch_shapes=[pltpu.VMEM((length, width), f32)],
        ),
        out_shape=[
            shape((length, feed_width // 2)),
            shape((length, feed_width // 2)),
            shape((8, feed_width), f32),
            shape((length, width), f32),
            shape((length, width)),
            shape((length, width // 2)),
            shape((length, width // 2)),
            shape((8, width), f32),
        ],
        compiler_params=params(56),
        name="feed_backward",
    )(core, grad_low, w_down, slope, w_up, hidden, normal, rstd, gain, wo)


def attend_back_kernel(core, expo, total, q, k, v, mix_t, grad_mixed, keep_out, send_out, sums_out):
    step = pl.program_id(0)
    steps = pl.num_programs(0)
    length = expo.shape[1]
    lanes = pl.ds(pl.multiple_of(step * 128, 128), 128)
    query = q[:, lanes]
    key_t = k[:, lanes].T
    value = v[:, lanes]
    grad_t = grad_mixed[:, lanes].astype(f32).T
    mix = mix_t[pl.ds(pl.multiple_of(step * 128, 128), 128), :]
    inverse = total[0, 0:2, :]
    scale = jnp.concatenate(
        [jnp.broadcast_to(inverse[0:1], (64, length)), jnp.broadcast_to(inverse[1:2], (64, length))], axis=0
    )
    scaled_t = (grad_t * scale).astype(bf16)
    scaled = scaled_t.T
    product = scaled_t.astype(f32) * mix
    grads_q, grads_k, grads_v = [], [], []
    for half in range(2):
        at = slice(half * 64, half * 64 + 64)
        inner = jnp.sum(product[at], axis=0, keepdims=True)
        probs = expo[half]
        grad_probs = dot(value[:, at], scaled_t[at, :])
        grad_scores = (probs.astype(f32) * (grad_probs - inner)).astype(bf16)
        grads_v.append(dot(probs, scaled[:, at]))
        grads_k.append(dot(grad_scores, query[:, at]))
        grads_q.append(dot(key_t[at, :], grad_scores))
    grad_query = (jnp.concatenate(grads_q, axis=0).T * 0.125).astype(bf16)
    grad_key = jnp.concatenate(grads_k, axis=1).astype(bf16)
    grad_value = jnp.concatenate(grads_v, axis=1).astype(bf16)
    kept = (step // (steps // 2)) == core[0]

    @pl.when(kept)
    def _():
        keep_out[0] = grad_query
        keep_out[1] = grad_key
        keep_out[2] = grad_value

    @pl.when(jnp.logical_not(kept))
    def _():
        send_out[0] = grad_query
        send_out[1] = grad_key
        send_out[2] = grad_value

    sums_out[...] = jnp.concatenate(
        [
            jnp.sum(grad_query.astype(f32), axis=0, keepdims=True),
            jnp.sum(grad_value.astype(f32), axis=0, keepdims=True),
            jnp.zeros((6, 128), f32),
        ],
        axis=0,
    )


def attend_back(core, expo, total, q, k, v, mix_t, grad_mixed):
    heads, length, _ = expo.shape
    width = q.shape[1]
    pairs = heads // 2
    per = pairs // 2
    flat = whole((length, width))
    return pl.pallas_call(
        attend_back_kernel,
        grid_spec=pltpu.PrefetchScalarGridSpec(
            num_scalar_prefetch=1,
            grid=(pairs,),
            in_specs=[
                pl.BlockSpec((2, length, length), lambda i, c: (i, 0, 0)),
                pl.BlockSpec((1, 8, length), lambda i, c: (i, 0, 0)),
                flat,
                flat,
                flat,
                whole((width, length)),
                flat,
            ],
            out_specs=[
                pl.BlockSpec((3, length, 128), lambda i, c: (0, 0, jnp.clip(i - per * c[0], 0, per - 1))),
                pl.BlockSpec((3, length, 128), lambda i, c: (0, 0, jnp.clip(i - per * (1 - c[0]), 0, per - 1))),
                pl.BlockSpec((8, 128), lambda i, c: (0, i)),
            ],
        ),
        out_shape=[
            shape((3, length, width // 2)),
            shape((3, length, width // 2)),
            shape((8, width), f32),
        ],
        compiler_params=params(56),
        name="attend_backward",
    )(core, expo, total, q, k, v, mix_t, grad_mixed)


def input_grad_kernel(core, hidden, keep, send, wq, wk, wv, o0, o1, o2, o3):
    width = hidden.shape[1]
    half = width // 2
    part = o0.shape[0]
    mine = pl.ds(pl.multiple_of(core[0] * half, 128), half)
    other = pl.ds(pl.multiple_of((1 - core[0]) * half, 128), half)
    total = hidden[...]
    for at, weight in enumerate((wq, wk, wv)):
        total += dot(keep[at], weight[:, mine], 1, 1) + dot(send[at], weight[:, other], 1, 1)
    for at, out in enumerate((o0, o1, o2, o3)):
        out[...] = total[at * part : (at + 1) * part].astype(bf16)


def input_grad(core, hidden, keep, send, wq, wk, wv):
    length, width = hidden.shape
    part = length // 4
    vmem = pl.BlockSpec(memory_space=pltpu.VMEM)
    return pl.pallas_call(
        input_grad_kernel,
        in_specs=[pl.BlockSpec(memory_space=pltpu.SMEM)] + [vmem] * 6,
        out_specs=[vmem] * 4,
        out_shape=[shape((part, width))] * 4,
        compiler_params=params(40),
        name="input_gradient",
    )(core, hidden, keep, send, wq, wk, wv)


def down_weight_kernel(own, other, keep, got, out):
    out[...] = (dot(own[...], keep[...], 0, 0) + dot(other[...], got[...], 0, 0)).astype(bf16)


def down_weight(own, other, keep, got):
    length, feed_width = own.shape
    half = keep.shape[1]
    tile = 768
    return pl.pallas_call(
        down_weight_kernel,
        grid=(feed_width // tile,),
        in_specs=[pl.BlockSpec((length, tile), lambda i: (0, i))] * 2 + [whole((length, half))] * 2,
        out_specs=pl.BlockSpec((tile, half), lambda i: (i, 0)),
        out_shape=shape((feed_width, half)),
        compiler_params=params(40),
        name="down_weight",
    )(own, other, keep, got)


def up_weight_kernel(own, other, keep, got, mix, mix_other, keep_b, got_b, first, second, out_w):
    step = pl.program_id(0)
    steps = pl.num_programs(0)
    value = (dot(own[...], keep[...], 0, 0) + dot(other[...], got[...], 0, 0)).astype(bf16)

    @pl.when(step < steps // 2)
    def _():
        first[...] = value

    @pl.when(step >= steps // 2)
    def _():
        second[...] = value

    @pl.when(step == 0)
    def _():
        out_w[...] = (dot(mix[...], keep_b[...], 0, 0) + dot(mix_other[...], got_b[...], 0, 0)).astype(bf16)


def up_weight(own, other, keep, got, mix, mix_other, keep_b, got_b):
    length, width = own.shape
    cols = keep.shape[1]
    tile = 384
    steps = cols // tile
    flat = whole((length, width))
    moving = pl.BlockSpec((length, tile), lambda i: (0, i))
    half = whole((length, width // 2))
    return pl.pallas_call(
        up_weight_kernel,
        grid=(steps,),
        in_specs=[flat, flat, moving, moving, flat, flat, half, half],
        out_specs=[
            pl.BlockSpec((width, tile), lambda i: (0, jnp.minimum(i, steps // 2 - 1))),
            pl.BlockSpec((width, tile), lambda i: (0, jnp.maximum(i - steps // 2, 0))),
            whole_out((width, width // 2)),
        ],
        out_shape=[shape((width, cols // 2)), shape((width, cols // 2)), shape((width, width // 2))],
        compiler_params=params(40),
        name="up_weight",
    )(own, other, keep, got, mix, mix_other, keep_b, got_b)


def head_weight_kernel(own, other, keep, got, out_q, out_kv):
    half = out_q.shape[1]
    left, right = own[...], other[...]
    out_q[...] = (dot(left, keep[0], 0, 0) + dot(right, got[0], 0, 0)).astype(bf16)
    for at in (1, 2):
        value = dot(left, keep[at], 0, 0) + dot(right, got[at], 0, 0)
        out_kv[:, (at - 1) * half : at * half] = value.astype(bf16)


def head_weight(own, other, keep, got):
    width = own.shape[1]
    vmem = pl.BlockSpec(memory_space=pltpu.VMEM)
    return pl.pallas_call(
        head_weight_kernel,
        in_specs=[vmem] * 4,
        out_specs=[vmem] * 2,
        out_shape=[shape((width, width // 2)), shape((width, width))],
        compiler_params=params(40),
        name="head_weight",
    )(own, other, keep, got)


def place_kernel(seq_at, b0, b1, b2, b3, out):
    for at, block in enumerate((b0, b1, b2, b3)):
        out[seq_at[0] ^ at] = block[...]


def place(seq_at, blocks):
    vmem = pl.BlockSpec(memory_space=pltpu.VMEM)
    return pl.pallas_call(
        place_kernel,
        in_specs=[pl.BlockSpec(memory_space=pltpu.SMEM)] + [vmem] * 4,
        out_specs=vmem,
        out_shape=shape((4, *blocks[0].shape)),
        compiler_params=params(16),
        name="place_rows",
    )(seq_at, *blocks)


def swap_seq(value, mask):
    return lax.ppermute(value, "seq", [(at, at ^ mask) for at in range(4)])


def reduce_part(value, order, row_at, seq_at, row_count):
    bits = row_count.bit_length() - 1
    value = value.reshape((2,) * bits + value.shape[1:])
    names = [1 << at for at in reversed(range(bits))] + ["x"]
    for axis in order:
        dim = names.index(axis)
        names.pop(dim)
        if axis == "x":
            bit = (seq_at >> 1) & 1
        else:
            bit = (row_at // axis) & 1
        keep = lax.dynamic_index_in_dim(value, bit, dim, keepdims=False)
        send = lax.dynamic_index_in_dim(value, 1 - bit, dim, keepdims=False)
        if axis == "x":
            got = swap_seq(send, 2)
        else:
            got = lax.ppermute(send, "rows", [(at, at ^ axis) for at in range(row_count)])
        value = (keep.astype(f32) + got.astype(f32)).astype(bf16)
    return value


def order_pair(bit, own, got):
    return jnp.where(bit == 0, own, got), jnp.where(bit == 0, got, own)


def local(
    row_count,
    tokens, segment_ids, w_query, w_key, w_value, b_query, b_value, w_out, b_out, gain_attn, shift_attn,
    w_up, b_up, w_down, b_down, gain_out, shift_out, token_cot, pool_cot,
):
    part, width = tokens.shape[1:]
    feed_width = w_up.shape[1]
    seq_at = lax.axis_index("seq")
    row_at = lax.axis_index("rows")
    core = (seq_at & 1).reshape(1)
    where_at = seq_at.reshape(1)

    def vec(v):
        return v.reshape(1, -1)

    ids = jnp.pad(segment_ids.astype(bf16)[:, None, :], ((0, 0), (0, 15), (0, width - part)))

    def token_block(mask):
        at = seq_at ^ mask
        return jnp.concatenate(
            [
                lax.dynamic_index_in_dim(tokens, at, 0, keepdims=False),
                lax.dynamic_index_in_dim(ids, at, 0, keepdims=False),
            ],
            axis=0,
        )

    def cot_block(mask):
        return lax.dynamic_index_in_dim(token_cot, seq_at ^ mask, 0, keepdims=False)

    blocks = [token_block(0)] + [swap_seq(token_block(mask), mask) for mask in (1, 2, 3)]
    cots = [cot_block(0)] + [swap_seq(cot_block(mask), mask) for mask in (1, 2, 3)]
    row_pool_cot = lax.dynamic_index_in_dim(pool_cot, seq_at, 0, keepdims=False)

    expo, total, row, q, k, v, mix_t, mixed, normal, rstd, low, ids_row = attend(
        blocks, w_query, w_key, w_value, w_out, vec(b_query), vec(b_value), vec(b_out), vec(gain_attn), vec(shift_attn)
    )
    row_other, mixed_other, low_other = swap_seq(row, 1), swap_seq(mixed, 1), swap_seq(low, 1)
    active, slope, l0, l1, l2, l3, pooled, hidden_two, keep_d, send_d, grad_down, sums_two = feed(
        core, low, w_up, vec(b_up), w_down, normal, vec(gain_attn), vec(shift_attn), vec(b_down),
        vec(gain_out), vec(shift_out), cots, ids_row, row_pool_cot,
    )
    active_other, got_d = swap_seq(active, 1), swap_seq(send_d, 1)
    layer_out = place(where_at, [l0] + [swap_seq(out, mask) for mask, out in ((1, l1), (2, l2), (3, l3))])
    pooled_all = lax.all_gather(pooled.astype(bf16), "seq", axis=0).astype(f32)

    keep_u, send_u, b_up_sum, hidden_one, grad_mixed, keep_b, send_b, sums_one = feed_back(
        core, grad_down, w_down, slope, w_up, hidden_two, normal, rstd, vec(gain_attn), w_out
    )
    got_u, got_b = swap_seq(send_u, 1), swap_seq(send_b, 1)
    grad_w_down = down_weight(active, active_other, keep_d, got_d)
    up_first, up_second, out_part = up_weight(low, low_other, keep_u, got_u, mixed, mixed_other, keep_b, got_b)
    keep_h, send_h, sums_head = attend_back(core, expo, total, q, k, v, mix_t, grad_mixed)
    got_h = swap_seq(send_h, 1)
    g0, g1, g2, g3 = input_grad(core, hidden_one, keep_h, send_h, w_query, w_key, w_value)
    query_part, key_value_part = head_weight(row, row_other, keep_h, got_h)
    grad_tokens = place(where_at, [g0] + [swap_seq(out, mask) for mask, out in ((1, g1), (2, g2), (3, g3))])

    shards = row_count
    bits = [1 << at for at in range(shards.bit_length() - 1)]
    order_a = ["x"] + bits
    order_b = [bits[0], "x"] + bits[1:]
    order_c = bits[1:] + [bits[0], "x"]
    half = width // 2
    rows = width // shards // 2
    vectors = jnp.concatenate(
        [
            b_up_sum[0].reshape(shards, -1),
            jnp.stack([sums_head[0], sums_head[1], sums_one[2], sums_one[0], sums_one[1], sums_two[2], sums_two[0], sums_two[1]])
            .reshape(8, shards, width // shards)
            .transpose(1, 0, 2)
            .reshape(shards, -1),
        ],
        axis=1,
    )
    count = vectors.shape[1]
    vec_rows = -(-count // (2 * half))
    vectors = jnp.pad(vectors, ((0, 0), (0, 2 * half * vec_rows - count))).reshape(shards, 2, vec_rows, half)
    vectors = jnp.pad(vectors, ((0, 0), (0, 0), (0, 16 - vec_rows), (0, 0))).astype(bf16)

    def cut(value):
        return value.reshape(shards, 2, -1, value.shape[1])

    query_all = jnp.concatenate([cut(query_part), vectors], axis=2)
    reduce = functools.partial(reduce_part, row_at=row_at, seq_at=seq_at, row_count=row_count)
    piece_d = reduce(cut(grad_w_down), order_b)
    piece_u1 = reduce(cut(up_first), order_a)
    piece_u2 = reduce(cut(up_second), order_c)
    piece_o = reduce(cut(out_part), order_c)
    piece_q = reduce(query_all, order_a)
    piece_kv = reduce(cut(key_value_part), order_b)
    feed_piece = jnp.concatenate(
        [piece_d, piece_u1[:, :half], piece_u1[:, half:], piece_u2[:, :half], piece_u2[:, half:]], axis=0
    )
    head_piece = jnp.concatenate([piece_o, piece_kv[:, :half], piece_kv[:, half:], piece_q], axis=0)

    def gather(piece):
        x_bit = (seq_at >> 1) & 1
        both = jnp.stack(order_pair(x_bit, piece, swap_seq(piece, 2)))
        other = swap_seq(both, 1)
        return both, other

    feed_own, feed_other = gather(feed_piece)
    head_own, head_other = gather(head_piece)
    core_bit = seq_at & 1

    def columns(own, other, at, count):
        left, right = order_pair(core_bit, own[:, at : at + count], other[:, at : at + count])
        left = left.reshape(2 * count, half)
        right = right.reshape(2 * count, half)
        return jnp.concatenate([left, right], axis=1).astype(f32)

    down_rows = piece_d.shape[0]
    out_w_down = columns(feed_own, feed_other, 0, down_rows)

    def up_columns(own, other):
        pieces = [own[:, down_rows + at * rows : down_rows + (at + 1) * rows].reshape(2 * rows, half) for at in range(4)]
        return jnp.concatenate(pieces, axis=1)

    left, right = order_pair(core_bit, up_columns(feed_own, None), up_columns(feed_other, None))
    out_w_up = jnp.concatenate([left, right], axis=1).astype(f32)
    out_w_out = columns(head_own, head_other, 0, rows)
    out_w_key = columns(head_own, head_other, rows, rows)
    out_w_value = columns(head_own, head_other, 2 * rows, rows)
    out_w_query = columns(head_own, head_other, 3 * rows, rows)
    at = 4 * rows
    vec_own = head_own[:, at : at + vec_rows].astype(f32) + head_other[:, at : at + vec_rows].astype(f32)
    vec_all = vec_own.reshape(-1)[:count]
    out_b_up = vec_all[: feed_width // shards]
    rest = vec_all[feed_width // shards :].reshape(8, width // shards)
    return (
        layer_out, pooled_all, grad_tokens,
        out_w_query, out_w_key, out_w_value, rest[0], rest[1], out_w_out, rest[2], rest[3], rest[4],
        out_w_up, out_b_up, out_w_down, rest[5], rest[6], rest[7],
    )


def solution(mesh):
    split = P("rows", "seq", None)
    in_specs = (split, P("rows", "seq"), *[P()] * 15, split, P("rows", None, None))
    mat, line = P("rows", None), P("rows")
    out_specs = (
        split, P("rows", None, None), split,
        mat, mat, mat, line, line, mat, line, line, line, mat, line, mat, line, line, line,
    )
    body = functools.partial(local, mesh.shape["rows"])
    return jax.shard_map(body, mesh=mesh, in_specs=in_specs, out_specs=out_specs, check_vma=False)
```

time: 992 us -> 285 us (0.29)
  waiting for transfers between devices: 677 us -> 103 us
  matrix products: 136 us -> 0 us
  Pallas kernels: 0 us -> 88.5 us
  starting transfers between devices: 0.67 us -> 45.4 us
  blocking collectives: 49.3 us -> 5.59 us
  local copies, waits for them, and re-layouts: 66 us -> 28.7 us
  other arithmetic: 47.3 us -> 11.5 us
  between operations: 16.4 us -> 1.6 us
    reduce_scatter x5 -> x0, waiting for transfers between devices: 401 us -> none  [the longest x1 165 us: local(): lax.psum_scatter(grad_w_up, 'rows', scatter_dimension=0, tiled=True)]
    unnamed x15 -> x0, waiting for transfers between devices: 211 us -> none
    dot_general x26 -> x0, matrix products: 136 us -> none  [the longest x6 40.1 us: matmul(): return jnp.dot(left, right, preferred_element_type=jnp.float32)]
    ppermute x0 -> x48, waiting for transfers between devices: none -> 103 us  [the longest x18 76.6 us: reduce_part(): lax.ppermute(send, 'rows', [(at, at ^ axis) for at in range(row_count)])]
    pallas_call x0 -> x10, Pallas kernels: none -> 88.5 us  [the longest x1 18.9 us: feed(): pl.pallas_call(feed_kernel, grid=(hidden // tile,), in_specs=[pl.BlockSpe...]
    ppermute x0 -> x48, starting transfers between devices: none -> 45.4 us  [the longest x18 25.2 us: reduce_part(): lax.ppermute(send, 'rows', [(at, at ^ axis) for at in range(row_count)])]
    unnamed x1 -> x0, blocking collectives: 36.3 us -> none
    all_gather x2 -> x0, waiting for transfers between devices: 33.7 us -> none  [the longest x1 20.3 us: local(): lax.all_gather(key_rows, 'seq', axis=1, tiled=True)]
  transfers between devices with their start and end apart: 12 -> 48, of which waited for: 10 -> 20; matrix products, arithmetic and copies ran while one was open for 13% -> 8% of each run, Pallas kernels for 0% -> 18%
where the time goes in v1:
time: 285 us; the launch traced here: 284 us
  waiting for transfers between devices  103 us (36%)
  Pallas kernels  88.5 us (31%)
  starting transfers between devices  45.4 us (16%)
  local copies, waits for them, and re-layouts  28.7 us (10%)
  other arithmetic  11.5 us (4%)
  blocking collectives  5.59 us (2%)
    ppermute x18, waiting for transfers between devices, reduce_part(): lax.ppermute(send, 'rows', [(at, at ^ axis) for at in range(row_count)])  76.6 us
    ppermute x30, waiting for transfers between devices, swap_seq(): return lax.ppermute(value, 'seq', [(at, at ^ mask) for at in range(4)])  26.3 us
    ppermute x18, starting transfers between devices, reduce_part(): lax.ppermute(send, 'rows', [(at, at ^ axis) for at in range(row_count)])  25.2 us
    ppermute x30, starting transfers between devices, swap_seq(): return lax.ppermute(value, 'seq', [(at, at ^ mask) for at in range(4)])  20.1 us
    pallas_call x1, Pallas kernels, feed(): pl.pallas_call(feed_kernel, grid=(hidden // tile,), in_specs=[pl.BlockSpe...  18.9 us
    pallas_call x1, Pallas kernels, attend(): pl.pallas_call(attend_kernel, grid=(pairs,), in_specs=[whole((part, width...  17.6 us
    pallas_call x1, Pallas kernels, feed_back(): pl.pallas_call(feed_back_kernel, grid_spec=pltpu.PrefetchScalarGridSpec(n...  17.6 us
    pallas_call x1, Pallas kernels, attend_back(): pl.pallas_call(attend_back_kernel, grid_spec=pltpu.PrefetchScalarGridSpec...  12.5 us
  transfers between devices with their start and end apart: 48, of which 20 were waited for; matrix products, arithmetic and copies ran while one was open for 8% of the time, Pallas kernels for 18%

profile of v1, /device:TPU:0, one launch (start us, length us, event | category | flops | bytes accessed | tf_op | source)
XLA Modules:
  0.0 284.2 jit_solution(10331314793851738627)
XLA Ops:
  3.5 2.6 collective-permute-start.1
  17.4 17.6 %attend_forward.1 = (bf16[12,512,512]{2,1,0:T(8,128)(2,1)}, f32[6,8,512]{2,1,0:T(8,128)}, bf16[512,768]{1,0:T(8,128)(2,1)}, bf16[512,768]{1,0:T(8,128)(2,1)}, bf...) custom-call(bf16[144,768]{1,0:T(8,128)(2,1)} %pad_maximum_fusion.4.t, ...), custom_call_target="tpu_custom_call" | custom-call | tf_op jit(solution)/shard_map/attend_forward/pallas_call | solution.py:112
  35.8 18.9 %feed_forward.1 = (bf16[512,3072]{1,0:T(8,128)(2,1)}, bf16[512,3072]{1,0:T(8,128)(2,1)}, bf16[128,768]{1,0:T(8,128)(2,1)}, bf16[128,768]{1,0:T(8,128)(2,1)}, bf1...) custom-call(s32[1]{0:T(128)} %bitcast.1.core, ...), custom_call_target="tpu_custom_call" | custom-call | tf_op jit(solution)/shard_map/feed_forward/pallas_call | solution.py:243
  54.7 17.6 %feed_backward.1 = (bf16[512,1536]{1,0:T(8,128)(2,1)}, bf16[512,1536]{1,0:T(8,128)(2,1)}, f32[8,3072]{1,0:T(8,128)}, f32[512,768]{1,0:T(8,128)}, bf16[512,768]{1...) custom-call(s32[1]{0:T(128)} %bitcast.1.core, ...), custom_call_target="tpu_custom_call" | custom-call | tf_op jit(solution)/shard_map/feed_backward/pallas_call | solution.py:349
  72.6 12.5 %attend_backward.1 = (bf16[3,512,384]{2,1,0:T(8,128)(2,1)}, bf16[3,512,384]{2,1,0:T(8,128)(2,1)}, f32[8,768]{1,0:T(8,128)}) custom-call(s32[1]{0:T(128)} %bitcast.1.core, bf16[12,512,512]{2,1,0:T(8,128)(2,1)} %get-tuple-element.75.expo, f32[6,8,512]{2,1,0:T(8,128)} %get-tuple-element.76.total, bf16[512,768]{1,0:T(8,128)(2,1)} %get-tuple-element.77.q, ...), custom_call_target="tpu_custom_call" | custom-call | tf_op jit(solution)/shard_map/attend_backward/pallas_call | solution.py:452
  87.8 4.0 %input_gradient.1 = (bf16[128,768]{1,0:T(8,128)(2,1)S(1)}, bf16[128,768]{1,0:T(8,128)(2,1)S(1)}, bf16[128,768]{1,0:T(8,128)(2,1)S(1)}, bf16[128,768]{1,0:T(8,128)(2,1)S(1)}) custom-call(s32[1]{0:T(128)} %bitcast.1.core, f32[512,768]{1,0:T(8,128)S(1)} %copy-done.10, bf16[3,512,384]{2,1,0:T(8,128)(2,1)S(1)} %copy-done.5, ...), custom_call_target="tpu_custom_call" | custom-call | tf_op jit(solution)/shard_map/input_gradient/pallas_call | solution.py:499
  95.0 5.3 %collective-permute-done.10.b2 = bf16[128,768]{1,0:T(8,128)(2,1)S(1)} collective-permute-done((bf16[128,768]{1,0:T(8,128)(2,1)S(1)}, bf16[128,768]{1,0:T(8,128)(2,1)S(1)}, u32[]{:S(2)}, u32[]{:S(2)}) %collective-permute-start.10) | collective-permute-done | bytes 196640 | tf_op jit(solution)/shard_map/ppermute | solution.py:609
  117.5 5.6 %all-gather = bf16[32,1728]{1,0:T(8,128)(2,1)S(1)} all-gather(bf16[8,1728]{1,0:T(8,128)(2,1)S(1)} %convert_element_type.329), channel_id=2, replica_groups=mesh['rows'=8,'seq'=4] {'seq'}, dimensions={0}, use_global_device_ids=true | all-gather | bytes 138240 | tf_op jit(solution)/shard_map/all_gather | solution.py:681
  132.1 4.1 %head_weight.1 = (bf16[768,384]{1,0:T(8,128)(2,1)S(1)}, bf16[768,768]{1,0:T(8,128)(2,1)S(1)}) custom-call(bf16[512,768]{1,0:T(8,128)(2,1)} %get-tuple-element.94.own, bf16[512,768]{1,0:T(8,128)(2,1)} %collective-permute-done.20.other, bf16[3,512,384]{2,1,0:T(8,128)(2,1)S(1)} %copy-done.6, bf16[3,512,384]{2,1,0:T(8,128)(2,1)S(1)} %collective-permute-done.21.got), custom_call_target="tpu_custom_call" | custom-call | tf_op jit(solution)/shard_map/head_weight/pallas_call | solution.py:581
  140.0 6.2 %up_weight.1 = (bf16[768,768]{1,0:T(8,128)(2,1)S(1)}, bf16[768,768]{1,0:T(8,128)(2,1)S(1)}, bf16[768,384]{1,0:T(8,128)(2,1)S(1)}) custom-call(bf16[512,768]{1,0:T(8,128)(2,1)S(1)} %copy-done.7, bf16[512,768]{1,0:T(8,128)(2,1)S(1)} %collective-permute-done.12.other, bf16[512,1536]{1,0:T(8,128)(2,1)S(1)} %copy-done.9, ...), custom_call_target="tpu_custom_call" | custom-call | tf_op jit(solution)/shard_map/up_weight/pallas_call | solution.py:554
  149.2 4.6 %collective-permute-done.22 = bf16[2,2,2,48,768]{4,3,2,1,0:T(8,128)(2,1)S(1)} collective-permute-done((bf16[2,2,2,48,768]{4,3,2,1,0:T(8,128)(2,1)S(1)}, bf16[2,2,2,48,768]{4,3,2,1,0:T(8,128)(2,1)S(1)}, u32[]{:S(2)}, u32[]{:S(2)}) %collective-permute-start.22) | collective-permute-done | bytes 589856 | tf_op jit(solution)/shard_map/ppermute | solution.py:628
  155.5 4.3 %collective-permute-done.27 = bf16[2,2,64,384]{3,2,1,0:T(8,128)(2,1)S(1)} collective-permute-done((bf16[2,2,64,384]{3,2,1,0:T(8,128)(2,1)S(1)}, bf16[2,2,64,384]{3,2,1,0:T(8,128)(2,1)S(1)}, u32[]{:S(2)}, u32[]{:S(2)}) %collective-permute-start.27) | collective-permute-done | bytes 196640 | tf_op jit(solution)/shard_map/ppermute | solution.py:628
  161.5 6.2 %collective-permute-done.16 = bf16[2,2,2,48,384]{4,3,2,1,0:T(8,128)(2,1)S(1)} collective-permute-done((bf16[2,2,2,48,384]{4,3,2,1,0:T(8,128)(2,1)S(1)}, bf16[2,2,2,48,384]{4,3,2,1,0:T(8,128)(2,1)S(1)}, u32[]{:S(2)}, u32[]{:S(2)}) %collective-permute-start.16) | collective-permute-done | bytes 294944 | tf_op jit(solution)/shard_map/ppermute | solution.py:628
  169.4 3.0 %collective-permute-done.28 = bf16[2,64,384]{2,1,0:T(8,128)(2,1)S(1)} collective-permute-done((bf16[2,64,384]{2,1,0:T(8,128)(2,1)S(1)}, bf16[2,64,384]{2,1,0:T(8,128)(2,1)S(1)}, u32[]{:S(2)}, u32[]{:S(2)}) %collective-permute-start.28) | collective-permute-done | bytes 98336 | tf_op jit(solution)/shard_map/ppermute | solution.py:628
  172.4 3.2 %collective-permute-start.29 = (bf16[64,384]{1,0:T(8,128)(2,1)S(1)}, bf16[64,384]{1,0:T(8,128)(2,1)S(1)}, u32[]{:S(2)}, u32[]{:S(2)}) collective-permute-start(bf16[64,384]{1,0:T(8,128)(2,1)S(1)} %dynamic-slice_bitcast_fusion.29), channel_id=1, source_target_pairs={{0,16},{4,20},{8,24},{12,28},{16,0},{20,4},{24,8},{28,12},{1,17},{... | collective-permute-start | bytes 147464 | tf_op jit(solution)/shard_map/ppermute | solution.py:628
  175.6 4.6 %collective-permute-done.29 = bf16[64,384]{1,0:T(8,128)(2,1)S(1)} collective-permute-done((bf16[64,384]{1,0:T(8,128)(2,1)S(1)}, bf16[64,384]{1,0:T(8,128)(2,1)S(1)}, u32[]{:S(2)}, u32[]{:S(2)}) %collective-permute-start.29) | collective-permute-done | bytes 49184 | tf_op jit(solution)/shard_map/ppermute | solution.py:628
  181.2 6.7 %collective-permute-done.17 = bf16[2,2,48,384]{3,2,1,0:T(8,128)(2,1)S(1)} collective-permute-done((bf16[2,2,48,384]{3,2,1,0:T(8,128)(2,1)S(1)}, bf16[2,2,48,384]{3,2,1,0:T(8,128)(2,1)S(1)}, u32[]{:S(2)}, u32[]{:S(2)}) %collective-permute-start.17) | collective-permute-done | bytes 147488 | tf_op jit(solution)/shard_map/ppermute | solution.py:628
  188.6 6.4 %collective-permute-done.23 = bf16[2,2,48,768]{3,2,1,0:T(8,128)(2,1)S(1)} collective-permute-done((bf16[2,2,48,768]{3,2,1,0:T(8,128)(2,1)S(1)}, bf16[2,2,48,768]{3,2,1,0:T(8,128)(2,1)S(1)}, u32[]{:S(2)}, u32[]{:S(2)}) %collective-permute-start.23) | collective-permute-done | bytes 294944 | tf_op jit(solution)/shard_map/ppermute | solution.py:609
  195.6 3.7 %collective-permute-done.18 = bf16[2,48,384]{2,1,0:T(8,128)(2,1)S(1)} collective-permute-done((bf16[2,48,384]{2,1,0:T(8,128)(2,1)S(1)}, bf16[2,48,384]{2,1,0:T(8,128)(2,1)S(1)}, u32[]{:S(2)}, u32[]{:S(2)}) %collective-permute-start.18) | collective-permute-done | bytes 73760 | tf_op jit(solution)/shard_map/ppermute | solution.py:628
  200.1 3.3 %collective-permute-done.19 = bf16[48,384]{1,0:T(8,128)(2,1)S(1)} collective-permute-done((bf16[48,384]{1,0:T(8,128)(2,1)S(1)}, bf16[48,384]{1,0:T(8,128)(2,1)S(1)}, u32[]{:S(2)}, u32[]{:S(2)}) %collective-permute-start.19) | collective-permute-done | bytes 36896 | tf_op jit(solution)/shard_map/ppermute | solution.py:609
  203.6 2.5 collective-permute-start.43
  206.1 4.0 %collective-permute-done.24 = bf16[2,48,768]{2,1,0:T(8,128)(2,1)S(1)} collective-permute-done((bf16[2,48,768]{2,1,0:T(8,128)(2,1)S(1)}, bf16[2,48,768]{2,1,0:T(8,128)(2,1)S(1)}, u32[]{:S(2)}, u32[]{:S(2)}) %collective-permute-start.24) | collective-permute-done | bytes 147488 | tf_op jit(solution)/shard_map/ppermute | solution.py:628
  210.4 5.7 %collective-permute-done.25 = bf16[48,768]{1,0:T(8,128)(2,1)S(1)} collective-permute-done((bf16[48,768]{1,0:T(8,128)(2,1)S(1)}, bf16[48,768]{1,0:T(8,128)(2,1)S(1)}, u32[]{:S(2)}, u32[]{:S(2)}) %collective-permute-start.25) | collective-permute-done | bytes 73760 | tf_op jit(solution)/shard_map/ppermute | solution.py:628
  216.9 4.5 %down_weight.1 = bf16[3072,384]{1,0:T(8,128)(2,1)S(1)} custom-call(bf16[512,3072]{1,0:T(8,128)(2,1)S(1)} %copy-done.8, bf16[512,3072]{1,0:T(8,128)(2,1)S(1)} %collective-permute-done.32.other, bf16[512,384]{1,0:T(8,128)(2,1)S(1)} %copy-done.12, bf16[512,384]{1,0:T(8,128)(2,1)S(1)} %collective-permute-done.33.got), custom_call_target="tpu_custom_call" | custom-call | tf_op jit(solution)/shard_map/down_weight/pallas_call | solution.py:517
  224.7 22.2 %collective-permute-done.39 = bf16[2,2,48,768]{3,2,0,1:T(8,128)(2,1)S(1)} collective-permute-done((bf16[2,2,48,768]{3,2,0,1:T(8,128)(2,1)S(1)}, bf16[2,2,48,768]{3,2,0,1:T(8,128)(2,1)S(1)}, u32[]{:S(2)}, u32[]{:S(2)}) %collective-permute-start.39) | collective-permute-done | bytes 294944 | tf_op jit(solution)/shard_map/ppermute | solution.py:628
  250.0 2.2 collective-permute-done.40
  252.3 2.3 collective-permute-start.41
  254.5 2.9 %collective-permute-done.35 = bf16[2,2,192,384]{3,2,1,0:T(8,128)(2,1)S(1)} collective-permute-done((bf16[2,2,192,384]{3,2,1,0:T(8,128)(2,1)S(1)}, bf16[2,2,192,384]{3,2,1,0:T(8,128)(2,1)S(1)}, u32[]{:S(2)}, u32[]{:S(2)}) %collective-permute-start.35) | collective-permute-done | bytes 589856 | tf_op jit(solution)/shard_map/ppermute | solution.py:609
  259.8 4.7 %collective-permute-done.36 = bf16[2,192,384]{2,1,0:T(8,128)(2,1)S(1)} collective-permute-done((bf16[2,192,384]{2,1,0:T(8,128)(2,1)S(1)}, bf16[2,192,384]{2,1,0:T(8,128)(2,1)S(1)}, u32[]{:S(2)}, u32[]{:S(2)}) %collective-permute-start.36) | collective-permute-done | bytes 294944 | tf_op jit(solution)/shard_map/ppermute | solution.py:628
  264.6 3.0 %collective-permute-start.37 = (bf16[192,384]{1,0:T(8,128)(2,1)S(1)}, bf16[192,384]{1,0:T(8,128)(2,1)S(1)}, u32[]{:S(2)}, u32[]{:S(2)}) collective-permute-start(bf16[192,384]{1,0:T(8,128)(2,1)S(1)} %dynamic-slice_bitcast_fusion.20), channel_id=1, source_target_pairs={{0,16},{4,20},{8,24},{12,28},{16,0},{20,4},{24,8},{28,12},{1,17},{... | collective-permute-start | bytes 442376 | tf_op jit(solution)/shard_map/ppermute | solution.py:628
  267.6 4.7 %collective-permute-done.37 = bf16[192,384]{1,0:T(8,128)(2,1)S(1)} collective-permute-done((bf16[192,384]{1,0:T(8,128)(2,1)S(1)}, bf16[192,384]{1,0:T(8,128)(2,1)S(1)}, u32[]{:S(2)}, u32[]{:S(2)}) %collective-permute-start.37) | collective-permute-done | bytes 147488 | tf_op jit(solution)/shard_map/ppermute | solution.py:628
  274.5 4.7 %collective-permute-done.46 = bf16[384,384]{1,0:T(8,128)(2,1)S(1)} collective-permute-done((bf16[384,384]{1,0:T(8,128)(2,1)S(1)}, bf16[384,384]{1,0:T(8,128)(2,1)S(1)}, u32[]{:S(2)}, u32[]{:S(2)}) %collective-permute-start.46) | collective-permute-done | bytes 294944 | tf_op jit(solution)/shard_map/ppermute | solution.py:609
  (271 shorter events, 78.8 us)
Async XLA Ops:
  2.9 11.7 %collective-permute-start = (bf16[144,768]{1,0:T(8,128)(2,1)S(1)}, bf16[144,768]{1,0:T(8,128)(2,1)S(1)}, u32[]{:S(2)}, u32[]{:S(2)}) collective-permute-start(bf16[144,768]{1,0:T(8,128)(2,1)S(1)} %pad_maximum_fusion.5), channel_id=1, source_target_pairs={{0,1},{1,0},{2,3},{3,2},{4,5},{5,4},{6,7},{7,6},{8,9},{9,8},{10,11... | collective-permute-start | bytes 663560 | tf_op jit(solution)/shard_map/ppermute | solution.py:609
  3.5 11.7 %collective-permute-start.1 = (bf16[144,768]{1,0:T(8,128)(2,1)S(1)}, bf16[144,768]{1,0:T(8,128)(2,1)S(1)}, u32[]{:S(2)}, u32[]{:S(2)}) collective-permute-start(bf16[144,768]{1,0:T(8,128)(2,1)S(1)} %pad_maximum_fusion.6), channel_id=1, source_target_pairs={{0,2},{1,3},{2,0},{3,1},{4,6},{5,7},{6,4},{7,5},{8,10},{9,11},{10,... | collective-permute-start | bytes 663560 | tf_op jit(solution)/shard_map/ppermute | solution.py:609
  6.1 10.6 %collective-permute-start.2 = (bf16[144,768]{1,0:T(8,128)(2,1)S(1)}, bf16[144,768]{1,0:T(8,128)(2,1)S(1)}, u32[]{:S(2)}, u32[]{:S(2)}) collective-permute-start(bf16[144,768]{1,0:T(8,128)(2,1)S(1)} %pad_maximum_fusion.7), channel_id=1, source_target_pairs={{0,3},{1,2},{2,1},{3,0},{4,7},{5,6},{6,5},{7,4},{8,11},{9,10},{10,... | collective-permute-start | bytes 663560 | tf_op jit(solution)/shard_map/ppermute | solution.py:609
  7.0 28.0 %collective-permute-start.3 = (bf16[128,768]{1,0:T(8,128)(2,1)S(1)}, bf16[128,768]{1,0:T(8,128)(2,1)S(1)}, u32[]{:S(2)}, u32[]{:S(2)}) collective-permute-start(bf16[128,768]{1,0:T(8,128)(2,1)S(1)} %get-tuple-element.111), channel_id=1, source_target_pairs={{0,1},{1,0},{2,3},{3,2},{4,5},{5,4},{6,7},{7,6},{8,9},{9,8},{10,11... | collective-permute-start | bytes 589832 | tf_op jit(solution)/shard_map/ppermute | solution.py:609
  7.1 27.9 %collective-permute-start.4 = (bf16[128,768]{1,0:T(8,128)(2,1)S(1)}, bf16[128,768]{1,0:T(8,128)(2,1)S(1)}, u32[]{:S(2)}, u32[]{:S(2)}) collective-permute-start(bf16[128,768]{1,0:T(8,128)(2,1)S(1)} %get-tuple-element.113), channel_id=1, source_target_pairs={{0,2},{1,3},{2,0},{3,1},{4,6},{5,7},{6,4},{7,5},{8,10},{9,11},{10,... | collective-permute-start | bytes 589832 | tf_op jit(solution)/shard_map/ppermute | solution.py:609
  14.5 20.5 %collective-permute-start.5 = (bf16[128,768]{1,0:T(8,128)(2,1)S(1)}, bf16[128,768]{1,0:T(8,128)(2,1)S(1)}, u32[]{:S(2)}, u32[]{:S(2)}) collective-permute-start(bf16[128,768]{1,0:T(8,128)(2,1)S(1)} %get-tuple-element.110), channel_id=1, source_target_pairs={{0,3},{1,2},{2,1},{3,0},{4,7},{5,6},{6,5},{7,4},{8,11},{9,10},{10,... | collective-permute-start | bytes 589832 | tf_op jit(solution)/shard_map/ppermute | solution.py:609
  72.3 67.7 %collective-permute-start.13 = (bf16[512,1536]{1,0:T(8,128)(2,1)}, bf16[512,1536]{1,0:T(8,128)(2,1)S(1)}, u32[]{:S(2)}, u32[]{:S(2)}) collective-permute-start(bf16[512,1536]{1,0:T(8,128)(2,1)} %get-tuple-element.89), channel_id=1, source_target_pairs={{0,1},{1,0},{2,3},{3,2},{4,5},{5,4},{6,7},{7,6},{8,9},{9,8},{10,11... | collective-permute-start | bytes 4718600 | tf_op jit(solution)/shard_map/ppermute | solution.py:609
  92.5 7.7 %collective-permute-start.10 = (bf16[128,768]{1,0:T(8,128)(2,1)S(1)}, bf16[128,768]{1,0:T(8,128)(2,1)S(1)}, u32[]{:S(2)}, u32[]{:S(2)}) collective-permute-start(bf16[128,768]{1,0:T(8,128)(2,1)S(1)} %get-tuple-element.86), channel_id=1, source_target_pairs={{0,2},{1,3},{2,0},{3,1},{4,6},{5,7},{6,4},{7,5},{8,10},{9,11},{10,... | collective-permute-start | bytes 589832 | tf_op jit(solution)/shard_map/ppermute | solution.py:609
  94.5 8.7 %collective-permute-start.11 = (bf16[128,768]{1,0:T(8,128)(2,1)S(1)}, bf16[128,768]{1,0:T(8,128)(2,1)S(1)}, u32[]{:S(2)}, u32[]{:S(2)}) collective-permute-start(bf16[128,768]{1,0:T(8,128)(2,1)S(1)} %get-tuple-element.87), channel_id=1, source_target_pairs={{0,3},{1,2},{2,1},{3,0},{4,7},{5,6},{6,5},{7,4},{8,11},{9,10},{10,... | collective-permute-start | bytes 589832 | tf_op jit(solution)/shard_map/ppermute | solution.py:609
  94.5 37.6 %collective-permute-start.21 = (bf16[3,512,384]{2,1,0:T(8,128)(2,1)}, bf16[3,512,384]{2,1,0:T(8,128)(2,1)S(1)}, u32[]{:S(2)}, u32[]{:S(2)}) collective-permute-start(bf16[3,512,384]{2,1,0:T(8,128)(2,1)} %get-tuple-element.83.send), channel_id=1, source_target_pairs={{0,1},{1,0},{2,3},{3,2},{4,5},{5,4},{6,7},{7,6},{8,9},{9,8},{10,11... | collective-permute-start | bytes 3538952 | tf_op jit(solution)/shard_map/ppermute | solution.py:609
  94.7 9.6 %collective-permute-start.9 = (bf16[128,768]{1,0:T(8,128)(2,1)S(1)}, bf16[128,768]{1,0:T(8,128)(2,1)S(1)}, u32[]{:S(2)}, u32[]{:S(2)}) collective-permute-start(bf16[128,768]{1,0:T(8,128)(2,1)S(1)} %get-tuple-element.85), channel_id=1, source_target_pairs={{0,1},{1,0},{2,3},{3,2},{4,5},{5,4},{6,7},{7,6},{8,9},{9,8},{10,11... | collective-permute-start | bytes 589832 | tf_op jit(solution)/shard_map/ppermute | solution.py:609
  103.8 20.4 %collective-permute-start.20 = (bf16[512,768]{1,0:T(8,128)(2,1)}, bf16[512,768]{1,0:T(8,128)(2,1)}, u32[]{:S(2)}, u32[]{:S(2)}) collective-permute-start(bf16[512,768]{1,0:T(8,128)(2,1)} %get-tuple-element.94.own), channel_id=1, source_target_pairs={{0,1},{1,0},{2,3},{3,2},{4,5},{5,4},{6,7},{7,6},{8,9},{9,8},{10,11... | collective-permute-start | bytes 2359304 | tf_op jit(solution)/shard_map/ppermute | solution.py:609
  105.0 18.0 %collective-permute-start.7 = (bf16[128,768]{1,0:T(8,128)(2,1)}, bf16[128,768]{1,0:T(8,128)(2,1)}, u32[]{:S(2)}, u32[]{:S(2)}) collective-permute-start(bf16[128,768]{1,0:T(8,128)(2,1)} %get-tuple-element.67), channel_id=1, source_target_pairs={{0,2},{1,3},{2,0},{3,1},{4,6},{5,7},{6,4},{7,5},{8,10},{9,11},{10,... | collective-permute-start | bytes 589832 | tf_op jit(solution)/shard_map/ppermute | solution.py:609
  107.4 16.0 %collective-permute-start.8 = (bf16[128,768]{1,0:T(8,128)(2,1)}, bf16[128,768]{1,0:T(8,128)(2,1)}, u32[]{:S(2)}, u32[]{:S(2)}) collective-permute-start(bf16[128,768]{1,0:T(8,128)(2,1)} %get-tuple-element.68), channel_id=1, source_target_pairs={{0,3},{1,2},{2,1},{3,0},{4,7},{5,6},{6,5},{7,4},{8,11},{9,10},{10,... | collective-permute-start | bytes 589832 | tf_op jit(solution)/shard_map/ppermute | solution.py:609
  123.0 14.9 %collective-permute-start.12 = (bf16[512,768]{1,0:T(8,128)(2,1)S(1)}, bf16[512,768]{1,0:T(8,128)(2,1)S(1)}, u32[]{:S(2)}, u32[]{:S(2)}) collective-permute-start(bf16[512,768]{1,0:T(8,128)(2,1)S(1)} %copy-done.7), channel_id=1, source_target_pairs={{0,1},{1,0},{2,3},{3,2},{4,5},{5,4},{6,7},{7,6},{8,9},{9,8},{10,11... | collective-permute-start | bytes 2359304 | tf_op jit(solution)/shard_map/ppermute | solution.py:609
  123.4 15.0 %collective-permute-start.14 = (bf16[512,768]{1,0:T(8,128)(2,1)}, bf16[512,768]{1,0:T(8,128)(2,1)S(1)}, u32[]{:S(2)}, u32[]{:S(2)}) collective-permute-start(bf16[512,768]{1,0:T(8,128)(2,1)} %get-tuple-element.90.mix), channel_id=1, source_target_pairs={{0,1},{1,0},{2,3},{3,2},{4,5},{5,4},{6,7},{7,6},{8,9},{9,8},{10,11... | collective-permute-start | bytes 2359304 | tf_op jit(solution)/shard_map/ppermute | solution.py:609
  124.3 13.6 %collective-permute-start.15 = (bf16[512,384]{1,0:T(8,128)(2,1)}, bf16[512,384]{1,0:T(8,128)(2,1)S(1)}, u32[]{:S(2)}, u32[]{:S(2)}) collective-permute-start(bf16[512,384]{1,0:T(8,128)(2,1)} %get-tuple-element.92), channel_id=1, source_target_pairs={{0,1},{1,0},{2,3},{3,2},{4,5},{5,4},{6,7},{7,6},{8,9},{9,8},{10,11... | collective-permute-start | bytes 1179656 | tf_op jit(solution)/shard_map/ppermute | solution.py:609
  136.4 11.7 %collective-permute-start.26 = (bf16[2,2,2,64,384]{4,3,2,1,0:T(8,128)(2,1)S(1)}, bf16[2,2,2,64,384]{4,3,2,1,0:T(8,128)(2,1)S(1)}, u32[]{:S(2)}, u32[]{:S(2)}) collective-permute-start(bf16[2,2,2,64,384]{4,3,2,1,0:T(8,128)(2,1)S(1)} %fusion.12), channel_id=1, source_target_pairs={{0,2},{1,3},{2,0},{3,1},{4,6},{5,7},{6,4},{7,5},{8,10},{9,11},{10,... | collective-permute-start | bytes 1179656 | tf_op jit(solution)/shard_map/ppermute | solution.py:609
  137.9 79.0 %collective-permute-start.32 = (bf16[512,3072]{1,0:T(8,128)(2,1)S(1)}, bf16[512,3072]{1,0:T(8,128)(2,1)S(1)}, u32[]{:S(2)}, u32[]{:S(2)}) collective-permute-start(bf16[512,3072]{1,0:T(8,128)(2,1)S(1)} %copy-done.8), channel_id=1, source_target_pairs={{0,1},{1,0},{2,3},{3,2},{4,5},{5,4},{6,7},{7,6},{8,9},{9,8},{10,11... | collective-permute-start | bytes 9437192 | tf_op jit(solution)/shard_map/ppermute | solution.py:609
  138.0 78.9 %collective-permute-start.33 = (bf16[512,384]{1,0:T(8,128)(2,1)S(1)}, bf16[512,384]{1,0:T(8,128)(2,1)S(1)}, u32[]{:S(2)}, u32[]{:S(2)}) collective-permute-start(bf16[512,384]{1,0:T(8,128)(2,1)S(1)} %copy-done.40), channel_id=1, source_target_pairs={{0,1},{1,0},{2,3},{3,2},{4,5},{5,4},{6,7},{7,6},{8,9},{9,8},{10,11... | collective-permute-start | bytes 1179656 | tf_op jit(solution)/shard_map/ppermute | solution.py:609
  138.5 15.3 %collective-permute-start.22 = (bf16[2,2,2,48,768]{4,3,2,1,0:T(8,128)(2,1)S(1)}, bf16[2,2,2,48,768]{4,3,2,1,0:T(8,128)(2,1)S(1)}, u32[]{:S(2)}, u32[]{:S(2)}) collective-permute-start(bf16[2,2,2,48,768]{4,3,2,1,0:T(8,128)(2,1)S(1)} %dynamic-slice_bitcast_fusion.3), channel_id=1, source_target_pairs={{0,4},{4,0},{8,12},{12,8},{16,20},{20,16},{24,28},{28,24},{1,5},{5... | collective-permute-start | bytes 1769480 | tf_op jit(solution)/shard_map/ppermute | solution.py:628
  146.3 57.1 %collective-permute-start.42 = (bf16[2,2,2,48,768]{4,3,2,1,0:T(8,128)(2,1)S(1)}, bf16[2,2,2,48,768]{4,3,2,1,0:T(8,128)(2,1)S(1)}, u32[]{:S(2)}, u32[]{:S(2)}) collective-permute-start(bf16[2,2,2,48,768]{4,3,2,1,0:T(8,128)(2,1)S(1)} %dynamic-slice_bitcast_fusion.1), channel_id=1, source_target_pairs={{0,8},{4,12},{8,0},{12,4},{16,24},{20,28},{24,16},{28,20},{1,9},{5... | collective-permute-start | bytes 1769480 | tf_op jit(solution)/shard_map/ppermute | solution.py:628
  148.1 62.1 %collective-permute-start.38 = (bf16[2,2,2,48,768]{4,3,0,1,2:T(8,128)(2,1)S(1)}, bf16[2,2,2,48,768]{4,3,0,1,2:T(8,128)(2,1)S(1)}, u32[]{:S(2)}, u32[]{:S(2)}) collective-permute-start(bf16[2,2,2,48,768]{4,3,0,1,2:T(8,128)(2,1)S(1)} %bitcast.219), channel_id=1, source_target_pairs={{0,2},{1,3},{2,0},{3,1},{4,6},{5,7},{6,4},{7,5},{8,10},{9,11},{10,... | collective-permute-start | bytes 1769480 | tf_op jit(solution)/shard_map/ppermute | solution.py:609
  159.9 7.9 %collective-permute-start.16 = (bf16[2,2,2,48,384]{4,3,2,1,0:T(8,128)(2,1)S(1)}, bf16[2,2,2,48,384]{4,3,2,1,0:T(8,128)(2,1)S(1)}, u32[]{:S(2)}, u32[]{:S(2)}) collective-permute-start(bf16[2,2,2,48,384]{4,3,2,1,0:T(8,128)(2,1)S(1)} %dynamic-slice_bitcast_fusion.8), channel_id=1, source_target_pairs={{0,8},{4,12},{8,0},{12,4},{16,24},{20,28},{24,16},{28,20},{1,9},{5... | collective-permute-start | bytes 884744 | tf_op jit(solution)/shard_map/ppermute | solution.py:628
  172.4 7.8 %collective-permute-start.29 = (bf16[64,384]{1,0:T(8,128)(2,1)S(1)}, bf16[64,384]{1,0:T(8,128)(2,1)S(1)}, u32[]{:S(2)}, u32[]{:S(2)}) collective-permute-start(bf16[64,384]{1,0:T(8,128)(2,1)S(1)} %dynamic-slice_bitcast_fusion.29), channel_id=1, source_target_pairs={{0,16},{4,20},{8,24},{12,28},{16,0},{20,4},{24,8},{28,12},{1,17},{... | collective-permute-start | bytes 147464 | tf_op jit(solution)/shard_map/ppermute | solution.py:628
  203.6 20.3 %collective-permute-start.43 = (bf16[2,2,48,768]{3,2,1,0:T(8,128)(2,1)S(1)}, bf16[2,2,48,768]{3,2,1,0:T(8,128)(2,1)S(1)}, u32[]{:S(2)}, u32[]{:S(2)}) collective-permute-start(bf16[2,2,48,768]{3,2,1,0:T(8,128)(2,1)S(1)} %dynamic-slice_bitcast_fusion.4), channel_id=1, source_target_pairs={{0,16},{4,20},{8,24},{12,28},{16,0},{20,4},{24,8},{28,12},{1,17},{... | collective-permute-start | bytes 884744 | tf_op jit(solution)/shard_map/ppermute | solution.py:628
  221.5 25.6 %collective-permute-start.34 = (bf16[2,2,2,192,384]{4,3,2,1,0:T(8,128)(2,1)S(1)}, bf16[2,2,2,192,384]{4,3,2,1,0:T(8,128)(2,1)S(1)}, u32[]{:S(2)}, u32[]{:S(2)}) collective-permute-start(bf16[2,2,2,192,384]{4,3,2,1,0:T(8,128)(2,1)S(1)} %dynamic-slice_bitcast_fusion), channel_id=1, source_target_pairs={{0,4},{4,0},{8,12},{12,8},{16,20},{20,16},{24,28},{28,24},{1,5},{5... | collective-permute-start | bytes 3538952 | tf_op jit(solution)/shard_map/ppermute | solution.py:628
  222.2 24.7 %collective-permute-start.39 = (bf16[2,2,48,768]{3,2,0,1:T(8,128)(2,1)S(1)}, bf16[2,2,48,768]{3,2,0,1:T(8,128)(2,1)S(1)}, u32[]{:S(2)}, u32[]{:S(2)}) collective-permute-start(bf16[2,2,48,768]{3,2,0,1:T(8,128)(2,1)S(1)} %dynamic-slice_bitcast_fusion.5), channel_id=1, source_target_pairs={{0,4},{4,0},{8,12},{12,8},{16,20},{20,16},{24,28},{28,24},{1,5},{5... | collective-permute-start | bytes 884744 | tf_op jit(solution)/shard_map/ppermute | solution.py:628
  223.8 43.7 %collective-permute-start.31 = (bf16[2,208,384]{2,1,0:T(8,128)(2,1)S(1)}, bf16[2,208,384]{2,1,0:T(8,128)(2,1)S(1)}, u32[]{:S(2)}, u32[]{:S(2)}) collective-permute-start(bf16[2,208,384]{2,1,0:T(8,128)(2,1)S(1)} %pad_maximum_fusion.1), channel_id=1, source_target_pairs={{0,1},{1,0},{2,3},{3,2},{4,5},{5,4},{6,7},{7,6},{8,9},{9,8},{10,11... | collective-permute-start | bytes 958472 | tf_op jit(solution)/shard_map/ppermute | solution.py:609
  224.0 24.9 %collective-permute-start.44 = (bf16[2,48,768]{2,1,0:T(8,128)(2,1)S(1)}, bf16[2,48,768]{2,1,0:T(8,128)(2,1)S(1)}, u32[]{:S(2)}, u32[]{:S(2)}) collective-permute-start(bf16[2,48,768]{2,1,0:T(8,128)(2,1)S(1)} %dynamic-slice_bitcast_fusion.18), channel_id=1, source_target_pairs={{0,4},{4,0},{8,12},{12,8},{16,20},{20,16},{24,28},{28,24},{1,5},{5... | collective-permute-start | bytes 442376 | tf_op jit(solution)/shard_map/ppermute | solution.py:628
  247.5 9.9 %collective-permute-start.35 = (bf16[2,2,192,384]{3,2,1,0:T(8,128)(2,1)S(1)}, bf16[2,2,192,384]{3,2,1,0:T(8,128)(2,1)S(1)}, u32[]{:S(2)}, u32[]{:S(2)}) collective-permute-start(bf16[2,2,192,384]{3,2,1,0:T(8,128)(2,1)S(1)} %dynamic-slice_bitcast_fusion.2), channel_id=1, source_target_pairs={{0,2},{1,3},{2,0},{3,1},{4,6},{5,7},{6,4},{7,5},{8,10},{9,11},{10,... | collective-permute-start | bytes 1769480 | tf_op jit(solution)/shard_map/ppermute | solution.py:609
  249.0 10.7 %collective-permute-start.45 = (bf16[48,768]{1,0:T(8,128)(2,1)S(1)}, bf16[48,768]{1,0:T(8,128)(2,1)S(1)}, u32[]{:S(2)}, u32[]{:S(2)}) collective-permute-start(bf16[48,768]{1,0:T(8,128)(2,1)S(1)} %dynamic-slice_bitcast_fusion.24), channel_id=1, source_target_pairs={{0,2},{1,3},{2,0},{3,1},{4,6},{5,7},{6,4},{7,5},{8,10},{9,11},{10,... | collective-permute-start | bytes 221192 | tf_op jit(solution)/shard_map/ppermute | solution.py:609
  (58 other events, 339.4 us)
